TPU v7x, 128 devices: a whole 4x4x4 slice. The times are simulated.
128 devices in a mesh: dp: 8 (over y, core), enc: 16 (over x, z).
Axes of the slice: x: 4, y: 4, z: 4, core: 2. Of those that a mesh axis runs over, the one named last changes fastest.
Arguments:
- hidden: bfloat16 [2048, 8192], P('dp', 'enc'), may hold values from -8 to 8
- encodings: bfloat16 [16, 128, 8192], P('dp', None, 'enc'), may hold values from -8 to 8
- query_weight: bfloat16 [8192, 4096], P('enc')
- key_weight: bfloat16 [8192, 4096], P('enc')
- value_weight: bfloat16 [8192, 4096], P('enc'), may hold values from -0.0625 to 0.0625
- out_weight: bfloat16 [4096, 8192], P(None, 'enc'), may hold values from -0.09375 to 0.09375
- out_cotangent: bfloat16 [2048, 8192], P('dp', 'enc'), may hold values from -6 to 6
- stretch_nbrs: int32 [32, 2], P('dp'), may hold values from 0 to 15, all different within a row
- nbr_blocks: int32 [16], replicated, may hold values from 1 to 8, as said below
Outputs:
- layer_out: float32 [2048, 8192], P('dp', 'enc')
- grad_hidden: float32 [2048, 8192], P('dp', 'enc')
- grad_encodings: float32 [16, 128, 8192], P('dp', None, 'enc')
- grad_query_weight: float32 [8192, 4096], P('enc', 'dp')
- grad_key_weight: float32 [8192, 4096], P('enc', 'dp')
- grad_value_weight: float32 [8192, 4096], P('enc', 'dp')
- grad_out_weight: float32 [4096, 8192], P('dp', 'enc')
Inputs may be any that keep to these rules, and one draw needn't show every extreme that they name: `stretch_nbrs`: each stretch names two different neighbours, and every neighbour is named by some stretch. Neighbour n holds 16 * nbr_blocks[n] valid token slots at its start; some neighbour is full.
All inputs are finite; a program needn't handle non-finite values.
Results may differ from a plain program's by a relative error of at most 0.022.
The roundings to bfloat16 on the way count: a program that leaves them out, or rounds other values in their place, can miss the bound.
Values may be sent and summed in bfloat16 or wider, within the bound.
A program may use at most 128 MiB of HBM per device.

v0:
```python
import jax
import jax.numpy as jnp
from jax import lax
from jax.sharding import PartitionSpec as P

HD = 128
BLK = 16


HIGH = lax.Precision.HIGHEST


def rounded(product_term):
    return lax.optimization_barrier(product_term.astype(jnp.bfloat16)).astype(jnp.float32)


def attend(queries, key_rows, value_rows, key_valid, score_scale):
    scores = (
        jnp.einsum("cthk,cjrhk->chjtr", queries, key_rows, preferred_element_type=jnp.float32)
        * score_scale
    )
    key_mask = key_valid[:, None, :, None, :]
    row_max = jnp.max(jnp.where(key_mask, scores, -1e30), axis=4)
    exp_terms = jnp.where(key_mask, jnp.exp(scores - row_max[..., None]), 0.0)
    row_total = jnp.sum(exp_terms, axis=4)
    partial_value = jnp.einsum(
        "chjtr,cjrhk->chjtk",
        exp_terms.astype(jnp.bfloat16),
        value_rows,
        preferred_element_type=jnp.float32,
    )
    best_max = jnp.max(row_max, axis=2, keepdims=True)
    factor = jnp.exp(row_max - best_max)
    denominator = jnp.sum(factor * row_total, axis=2)
    output = jnp.sum(factor[..., None] * partial_value, axis=2) / denominator[..., None]
    return (output, exp_terms, factor, denominator)


def attend_back(
    queries, key_rows, value_rows, score_scale, exp_terms, factor, denominator, grad_blocks
):
    weights = factor[..., None] * exp_terms / denominator[:, :, None, :, None]
    value_contrib = jnp.einsum(
        "chjtr,cthk->cjrhk",
        weights.astype(jnp.bfloat16),
        grad_blocks,
        preferred_element_type=jnp.float32,
    )
    grad_probs = jnp.einsum(
        "cthk,cjrhk->chjtr", grad_blocks, value_rows, preferred_element_type=jnp.float32
    )
    row_inner = jnp.sum(weights * grad_probs, axis=(2, 4), keepdims=True)
    grad_scores = (weights * (grad_probs - row_inner) * score_scale).astype(jnp.bfloat16)
    grad_q = jnp.einsum(
        "chjtr,cjrhk->cthk", grad_scores, key_rows, preferred_element_type=jnp.float32
    )
    key_contrib = jnp.einsum(
        "chjtr,cthk->cjrhk", grad_scores, queries, preferred_element_type=jnp.float32
    )
    return (grad_q, key_contrib, value_contrib)


def per_device(
    hidden,
    encodings,
    query_weight,
    key_weight,
    value_weight,
    out_weight,
    out_cotangent,
    stretch_nbrs,
    nbr_blocks,
):
    tok_rows, part_width = hidden.shape
    owned_nbrs, span_rows, _ = encodings.shape
    heads_width = query_weight.shape[1]
    stretches = stretch_nbrs.shape[0]
    neighbour_count = nbr_blocks.shape[0]
    score_scale = HD ** (-0.5)
    flat_enc = encodings.reshape(owned_nbrs * span_rows, part_width)
    query_part = rounded(jnp.dot(hidden, query_weight, preferred_element_type=jnp.float32))[None]
    pair_part = jnp.stack(
        [
            rounded(jnp.dot(flat_enc, key_weight, preferred_element_type=jnp.float32)),
            rounded(jnp.dot(flat_enc, value_weight, preferred_element_type=jnp.float32)),
        ]
    )
    query_sum, pair_sum = (
        lax.psum_scatter(query_part, "enc", scatter_dimension=2, tiled=True),
        lax.psum_scatter(pair_part, "enc", scatter_dimension=2, tiled=True),
    )
    queries = query_sum[0].astype(jnp.bfloat16)
    pair_own = pair_sum.astype(jnp.bfloat16)
    local_width = queries.shape[1]
    local_heads = local_width // HD
    onehot = stretch_nbrs[:, :, None] == jnp.arange(neighbour_count, dtype=jnp.int32)[None, None, :]
    limits = BLK * jnp.sum(jnp.where(onehot, nbr_blocks[None, None, :], 0), axis=2)
    key_valid = jnp.arange(span_rows, dtype=jnp.int32)[None, None, :] < limits[:, :, None]
    pair_all = lax.all_gather(pair_own, "dp", axis=1, tiled=True)
    pair_table = pair_all.reshape(2, neighbour_count, span_rows, local_heads, HD)
    picked = pair_table[:, stretch_nbrs]
    key_picked = picked[0]
    value_picked = picked[1]
    query_blocks = queries.reshape(stretches, tok_rows // stretches, local_heads, HD)
    output, exp_terms, factor, denominator = attend(
        query_blocks, key_picked, value_picked, key_valid, score_scale
    )
    heads_out = output.transpose(0, 2, 1, 3).reshape(tok_rows, local_width).astype(jnp.bfloat16)
    all_heads = lax.all_gather(heads_out, "enc", axis=1, tiled=True)
    layer_out = jnp.dot(all_heads, out_weight, preferred_element_type=jnp.float32)
    grad_part = lax.dot_general(
        out_cotangent, out_weight, (((1,), (1,)), ((), ())), preferred_element_type=jnp.float32
    )
    grad_heads = lax.psum_scatter(grad_part, "enc", scatter_dimension=1, tiled=True).astype(
        jnp.bfloat16
    )
    grad_out_weight = lax.psum_scatter(
        lax.dot_general(
            all_heads, out_cotangent, (((0,), (0,)), ((), ())), preferred_element_type=jnp.float32
        ).astype(jnp.bfloat16),
        "dp",
        scatter_dimension=0,
        tiled=True,
    ).astype(jnp.float32)
    grad_blocks = grad_heads.reshape(stretches, tok_rows // stretches, local_heads, HD)
    grad_q, key_contrib, value_contrib = attend_back(
        query_blocks,
        key_picked,
        value_picked,
        score_scale,
        exp_terms,
        factor,
        denominator,
        grad_blocks,
    )
    grad_query = grad_q.reshape(tok_rows, local_width).astype(jnp.bfloat16)
    grad_pair = jnp.stack([key_contrib, value_contrib]).reshape(
        2, stretches, 2, span_rows, local_width
    )
    dense_grads = jnp.einsum(
        "cjn,acjrk->anrk",
        onehot.astype(jnp.float32),
        grad_pair,
        precision=HIGH,
        preferred_element_type=jnp.float32,
    )
    home_sums = lax.psum_scatter(
        dense_grads.astype(jnp.bfloat16), "dp", scatter_dimension=1, tiled=True
    )
    all_pair_grads = lax.all_gather(home_sums, "enc", axis=3, tiled=True)
    flat_grads = all_pair_grads.reshape(2, owned_nbrs * span_rows, heads_width)
    enc_sum = lax.dot_general(
        flat_grads[0], key_weight, (((1,), (1,)), ((), ())), preferred_element_type=jnp.float32
    )
    enc_sum = enc_sum + lax.dot_general(
        flat_grads[1], value_weight, (((1,), (1,)), ((), ())), preferred_element_type=jnp.float32
    )
    grad_encodings = enc_sum.reshape(owned_nbrs, span_rows, part_width)
    all_query_grads = lax.all_gather(grad_query, "enc", axis=1, tiled=True)
    grad_hidden = lax.dot_general(
        all_query_grads, query_weight, (((1,), (1,)), ((), ())), preferred_element_type=jnp.float32
    )
    query_term = lax.dot_general(
        hidden, all_query_grads, (((0,), (0,)), ((), ())), preferred_element_type=jnp.float32
    )
    grad_query_weight = lax.psum_scatter(
        query_term.astype(jnp.bfloat16), "dp", scatter_dimension=1, tiled=True
    ).astype(jnp.float32)
    pair_terms = jnp.stack(
        [
            lax.dot_general(
                flat_enc,
                flat_grads[0],
                (((0,), (0,)), ((), ())),
                preferred_element_type=jnp.float32,
            ),
            lax.dot_general(
                flat_enc,
                flat_grads[1],
                (((0,), (0,)), ((), ())),
                preferred_element_type=jnp.float32,
            ),
        ]
    )
    pair_weight = lax.psum_scatter(
        pair_terms.astype(jnp.bfloat16), "dp", scatter_dimension=2, tiled=True
    ).astype(jnp.float32)
    grad_key_weight = pair_weight[0]
    grad_value_weight = pair_weight[1]
    return (
        layer_out,
        grad_hidden,
        grad_encodings,
        grad_query_weight,
        grad_key_weight,
        grad_value_weight,
        grad_out_weight,
    )


def solution(mesh):
    in_specs = (
        P("dp", "enc"),
        P("dp", None, "enc"),
        P("enc", None),
        P("enc", None),
        P("enc", None),
        P(None, "enc"),
        P("dp", "enc"),
        P("dp", None),
        P(),
    )
    out_specs = (
        P("dp", "enc"),
        P("dp", "enc"),
        P("dp", None, "enc"),
        P("enc", "dp"),
        P("enc", "dp"),
        P("enc", "dp"),
        P("dp", "enc"),
    )
    return jax.shard_map(
        per_device, mesh=mesh, in_specs=in_specs, out_specs=out_specs, check_vma=False
    )
```

profile of v0, /device:TPU:0, one launch (start us, length us, event | category | flops | bytes accessed | tf_op | source)
XLA Modules:
  0.0 646.2 jit_solution(18179898291554959961)
XLA Ops:
  7.2 0.9 copy-done
  8.1 3.6 convolution_convert_fusion.5
  11.7 1.3 convolution_convert_fusion.6
  13.0 3.8 maximum_convert_fusion
  16.9 0.9 copy-done.12
  17.7 3.4 convolution_convert_fusion.4
  21.2 2.5 bitcast_convert_fusion.1
  23.7 5.4 fusion.30
  29.2 75.1 %reduce-scatter.8.cloned.1.call-done = f32[2,256,256]{2,1,0:T(8,128)} async-done(((f32[2,256,4096]{2,1,0:T(8,128)}), f32[2,256,256]{2,1,0:T(8,128)}) %reduce-scatter.8.cloned.1.call-update) | async-done | bytes 524304 | tf_op jit(solution)/shard_map/reduce_scatter | solution.py:90
  104.3 1.8 convert_element_type.77
  106.1 0.2 reduce-scatter.14.cloned.1.call-start
  106.4 0.2 select_reduce_fusion.2
  107.0 77.8 %reduce-scatter.10.cloned.1.call-done = f32[1,256,256]{2,1,0:T(8,128)} async-done(((f32[1,256,4096]{2,1,0:T(8,128)}), f32[1,256,256]{2,1,0:T(8,128)}) %reduce-scatter.10.cloned.1.call-update) | async-done | bytes 262160 | tf_op jit(solution)/shard_map/reduce_scatter | solution.py:89
  184.8 1.0 convert_element_type.79
  185.8 79.8 %reduce-scatter.12.cloned.1.call-done = f32[256,256]{1,0:T(8,128)} async-done(((f32[256,4096]{1,0:T(8,128)}), f32[256,256]{1,0:T(8,128)}) %reduce-scatter.12.cloned.1.call-update) | async-done | bytes 262160 | tf_op jit(solution)/shard_map/reduce_scatter | solution.py:114
  265.6 1.0 convert_element_type.84
  266.5 0.7 reshape.62
  267.2 24.9 %all-gather.5.cloned.1.call-done = bf16[2,2048,256]{2,1,0:T(8,128)(2,1)} async-done(((bf16[2,256,256]{2,1,0:T(8,128)(2,1)}), bf16[2,2048,256]{2,1,0:T(8,128)(2,1)}) %all-gather.5.cloned.1.call-update) | async-done | bytes 2097168 | tf_op jit(solution)/shard_map/all_gather | solution.py:99
  292.2 2.5 reshape.61
  294.7 1.9 copy.64
  296.6 2.4 gather_fusion
  299.1 0.5 select_reduce_fusion
  299.6 0.4 bitcast_reduce_fusion
  300.1 1.3 multiply_reduce_fusion
  301.4 0.9 convolution_bitcast_fusion
  302.4 0.5 copy.75
  303.0 1.2 multiply_convert_fusion
  304.2 0.3 convolution_bitcast_fusion.1
  304.6 0.3 copy-done.6
  304.9 0.5 copy.74
  305.4 3.0 fusion.6
  308.4 2.1 copy.76
  310.5 0.3 fusion.9
  310.9 0.1 fusion.13
  311.2 0.7 copy.115
  311.9 0.2 fusion.11
  312.3 0.7 copy.114
  313.1 31.5 %reduce-scatter.14.cloned.1.call-done = bf16[2,2,128,256]{3,2,0,1:T(8,128)(2,1)} async-done(((bf16[2,16,128,256]{3,2,0,1:T(8,128)(2,1)}), bf16[2,2,128,256]{3,2,0,1:T(8,128)(2,1)}) %reduce-scatter.14.cloned.1.call-update) | async-done | bytes 262160 | tf_op jit(solution)/shard_map/reduce_scatter | solution.py:147
  344.5 1.7 copy.77
  346.3 47.4 %all-gather.7.cloned.1.call-done = bf16[256,4096]{1,0:T(8,128)(2,1)} async-done(((bf16[256,256]{1,0:T(8,128)(2,1)}), bf16[256,4096]{1,0:T(8,128)(2,1)}) %all-gather.7.cloned.1.call-update) | async-done | bytes 2097168 | tf_op jit(solution)/shard_map/all_gather | solution.py:109
  393.6 4.8 convolution_convert_fusion
  398.5 44.9 %all-gather.9.cloned.1.call-done = bf16[256,4096]{1,0:T(8,128)(2,1)} async-done(((bf16[256,256]{1,0:T(8,128)(2,1)}), bf16[256,4096]{1,0:T(8,128)(2,1)}) %all-gather.9.cloned.1.call-update) | async-done | bytes 2097168 | tf_op jit(solution)/shard_map/all_gather | solution.py:159
  443.4 4.9 fusion
  448.3 0.3 reduce-scatter.18.cloned.1.call-start
  448.6 54.5 %all-gather.11.cloned.1.call-done = bf16[2,2,128,4096]{3,2,1,0:T(8,128)(2,1)} async-done(((bf16[2,2,128,256]{3,2,1,0:T(8,128)(2,1)}), bf16[2,2,128,4096]{3,2,1,0:T(8,128)(2,1)}) %all-gather.11.cloned.1.call-update) | async-done | bytes 4194320 | tf_op jit(solution)/shard_map/all_gather | solution.py:150
  503.1 2.6 fusion.28
  505.7 1.3 fusion.2
  507.1 3.2 fusion.1
  510.3 6.2 pad_maximum_fusion
  516.5 5.1 fusion.29
  521.6 2.1 fusion.31
  523.7 1.0 copy-done.21
  524.7 1.3 fusion.32
  526.0 1.0 copy-done.22
  527.0 2.4 convolution_add_fusion
  529.4 13.3 %reduce-scatter.20.cloned.1.call-done = bf16[512,512]{1,0:T(8,128)(2,1)} async-done(((bf16[4096,512]{1,0:T(8,128)(2,1)}), bf16[512,512]{1,0:T(8,128)(2,1)}) %reduce-scatter.20.cloned.1.call-update) | async-done | bytes 524304 | tf_op jit(solution)/shard_map/reduce_scatter | solution.py:117
  542.7 2.1 convert_element_type.97
  544.9 36.7 %reduce-scatter.16.cloned.1.call-done = bf16[512,512]{0,1:T(8,128)(2,1)} async-done(((bf16[512,4096]{0,1:T(8,128)(2,1)}), bf16[512,512]{0,1:T(8,128)(2,1)}) %reduce-scatter.16.cloned.1.call-update) | async-done | bytes 524304 | tf_op jit(solution)/shard_map/reduce_scatter | solution.py:166
  581.6 2.2 copy.78
  583.8 51.6 %reduce-scatter.18.cloned.1.call-done = bf16[2,512,512]{1,2,0:T(8,128)(2,1)} async-done(((bf16[2,512,4096]{1,2,0:T(8,128)(2,1)}), bf16[2,512,512]{1,2,0:T(8,128)(2,1)}) %reduce-scatter.18.cloned.1.call-update) | async-done | bytes 1048592 | tf_op jit(solution)/shard_map/reduce_scatter | solution.py:185
  635.4 1.5 convert_element_type.95
  636.9 0.2 slice_bitcast_fusion
  637.1 1.3 copy.80
  638.4 1.3 copy.79
  (75 shorter events, 1.7 us)
Async XLA Ops:
  7.2 1.0 copy-start
  7.2 97.1 %reduce-scatter.8.cloned.1.call-start = ((), (), s32[]{:S(2)}) async-start(), calls=%async_computation.7 | async-start | bytes 8912896 | tf_op jit(solution)/shard_map/reduce_scatter | solution.py:90
  8.1 3.6 copy-start.20
  16.8 0.9 copy-start.12
  16.8 168.0 %reduce-scatter.10.cloned.1.call-start = ((), (), s32[]{:S(2)}) async-start(), calls=%async_computation.9 | async-start | bytes 4456448 | tf_op jit(solution)/shard_map/reduce_scatter | solution.py:89
  21.2 2.6 copy-start.10
  23.7 241.9 %reduce-scatter.12.cloned.1.call-start = ((), (), s32[]{:S(2)}) async-start(), calls=%async_computation.11 | async-start | bytes 4456448 | tf_op jit(solution)/shard_map/reduce_scatter | solution.py:114
  29.1 77.2 %copy-start.17 = (s32[4,2]{0,1:T(2,128)S(1)}, s32[4,2]{0,1:T(2,128)}, u32[]{:S(2)}) copy-start(s32[4,2]{0,1:T(2,128)} %param.16) | copy-start | bytes 100
  29.1 77.2 %copy-start.18 = (s32[16]{0:T(128)S(1)}, s32[16]{0:T(128)}, u32[]{:S(2)}) copy-start(s32[16]{0:T(128)} %param.17) | copy-start | bytes 196
  29.2 263.0 %all-gather.5.cloned.1.call-start = ((), (), s32[]{:S(2)}) async-start(), calls=%async_computation.8 | async-start | bytes 2359296 | tf_op jit(solution)/shard_map/all_gather | solution.py:99
  106.1 238.4 %reduce-scatter.14.cloned.1.call-start = ((), (), s32[]{:S(2)}) async-start(), calls=%async_computation.13 | async-start | bytes 2359296 | tf_op jit(solution)/shard_map/reduce_scatter | solution.py:147
  296.6 3.5 copy-start.14
  299.1 3.2 copy-start.4
  299.6 3.4 copy-start.8
  300.1 1.4 copy-start.15
  304.2 0.7 copy-start.6
  308.3 2.2 copy-start.5
  308.3 2.2 copy-start.9
  308.4 2.2 copy-start.16
  308.4 3.6 copy-start.7
  310.4 83.2 %copy-start.11 = (bf16[256,512]{1,0:T(8,128)(2,1)S(1)}, bf16[256,512]{1,0:T(8,128)(2,1)}, u32[]{:S(2)}) copy-start(bf16[256,512]{1,0:T(8,128)(2,1)} %param.15) | copy-start | bytes 786436
  310.5 83.2 %all-gather.7.cloned.1.call-start = ((), (), s32[]{:S(2)}) async-start(), calls=%async_computation.10 | async-start | bytes 2228224 | tf_op jit(solution)/shard_map/all_gather | solution.py:109
  311.9 131.5 %all-gather.9.cloned.1.call-start = ((), (), s32[]{:S(2)}) async-start(), calls=%async_computation.12 | async-start | bytes 2228224 | tf_op jit(solution)/shard_map/all_gather | solution.py:159
  313.0 190.1 %all-gather.11.cloned.1.call-start = ((), (), s32[]{:S(2)}) async-start(), calls=%async_computation.14 | async-start | bytes 4456448 | tf_op jit(solution)/shard_map/all_gather | solution.py:150
  346.2 196.5 %reduce-scatter.20.cloned.1.call-start = ((), (), s32[]{:S(2)}) async-start(), calls=%async_computation.17 | async-start | bytes 4718592 | tf_op jit(solution)/shard_map/reduce_scatter | solution.py:117
  398.4 45.0 %copy-start.13 = (bf16[256,512]{1,0:T(8,128)(2,1)S(1)}, bf16[256,512]{1,0:T(8,128)(2,1)}, u32[]{:S(2)}) copy-start(bf16[256,512]{1,0:T(8,128)(2,1)} %param.9) | copy-start | bytes 786436
  398.5 183.1 %reduce-scatter.16.cloned.1.call-start = ((), (), s32[]{:S(2)}) async-start(), calls=%async_computation.15 | async-start | bytes 4718592 | tf_op jit(solution)/shard_map/reduce_scatter | solution.py:166
  448.3 187.1 %reduce-scatter.18.cloned.1.call-start = ((), (), s32[]{:S(2)}) async-start(), calls=%async_computation.16 | async-start | bytes 9437184 | tf_op jit(solution)/shard_map/reduce_scatter | solution.py:185
  505.7 1.4 copy-start.1
  516.5 5.1 copy-start.3
  516.5 5.1 copy-start.19
  521.6 2.1 copy-start.2
  521.6 3.1 copy-start.21
  524.7 2.3 copy-start.22
Sparse Core Ops, SparseCore 0:
  16.9 87.3 reduce-scatter.7
  107.7 77.0 reduce-scatter.9
  188.5 77.0 reduce-scatter.11
  267.7 24.4 all-gather.4
  310.6 33.8 reduce-scatter.13
  347.1 46.5 all-gather.6
  396.3 47.0 all-gather.8
  446.1 56.9 all-gather.10
  505.5 37.1 reduce-scatter.19
  545.0 36.5 reduce-scatter.15
  584.0 51.3 reduce-scatter.17
where the time goes:
time: 647 us; the launch traced here: 646 us
  waiting for transfers between devices  538 us (83%)
  matrix products  45.4 us (7%)
  local copies, waits for them, and re-layouts  26.2 us (4%)
  other arithmetic  21.8 us (3%)
  between operations  14.3 us (2%)
    reduce_scatter x1, waiting for transfers between devices, per_device(): lax.psum_scatter(grad_part, 'enc', scatter_dimension=1, tiled=True)  79.8 us
    reduce_scatter x1, waiting for transfers between devices, per_device(): lax.psum_scatter(query_part, 'enc', scatter_dimension=2, tiled=True)  77.8 us
    reduce_scatter x1, waiting for transfers between devices, per_device(): lax.psum_scatter(pair_part, 'enc', scatter_dimension=2, tiled=True)  75.1 us
    all_gather x1, waiting for transfers between devices, per_device(): all_pair_grads = lax.all_gather(home_sums, 'enc', axis=3, tiled=True)  54.5 us
    reduce_scatter x1, waiting for transfers between devices, per_device(): lax.psum_scatter(pair_terms.astype(jnp.bfloat16), 'dp', scatter_dimension...  51.6 us
    all_gather x1, waiting for transfers between devices, per_device(): all_heads = lax.all_gather(heads_out, 'enc', axis=1, tiled=True)  47.4 us
    all_gather x1, waiting for transfers between devices, per_device(): all_query_grads = lax.all_gather(grad_query, 'enc', axis=1, tiled=True)  44.9 us
    reduce_scatter x1, waiting for transfers between devices, per_device(): lax.psum_scatter(query_term.astype(jnp.bfloat16), 'dp', scatter_dimension...  36.7 us
  transfers between devices with their start and end apart: 11, of which 11 were waited for; matrix products, arithmetic and copies ran while one was open for 9% of the time, Pallas kernels for 0%

commit v1 on v0

v1 whole, which is shorter than its diff:
```python
import functools

import jax
import jax.numpy as jnp
from jax import lax
from jax.experimental import pallas as pl
from jax.experimental.pallas import tpu as pltpu
from jax.sharding import PartitionSpec as P

HD = 128
BLK = 16
MESH = pl.DeviceIdType.MESH
F32 = jnp.float32
BF16 = jnp.bfloat16
NT = (((1,), (1,)), ((), ()))
TN = (((0,), (0,)), ((), ()))


def mm(a, b):
    return jnp.dot(a, b, preferred_element_type=F32)


class Place:
    def __init__(self):
        self.dp = lax.axis_index("dp")
        self.enc = lax.axis_index("enc")
        dp, enc = self.dp, self.enc
        self.y, self.c = dp // 2, dp % 2
        self.x, self.z = enc // 4, enc % 4
        x, y, z, c = self.x, self.y, self.z, self.c
        self.right = {
            "x": (dp, ((x + 1) % 4) * 4 + z),
            "z": (dp, x * 4 + (z + 1) % 4),
            "y": (((y + 1) % 4) * 2 + c, enc),
        }
        self.left = {
            "x": (dp, ((x + 3) % 4) * 4 + z),
            "z": (dp, x * 4 + (z + 3) % 4),
            "y": (((y + 3) % 4) * 2 + c, enc),
        }
        self.pos = {"x": x, "y": y, "z": z}
        self.partner = (y * 2 + (1 - c), enc)

    def barrier(self):
        sem = pltpu.get_barrier_semaphore()
        others = list(self.right.values()) + list(self.left.values()) + [self.partner]
        for other in others:
            pl.semaphore_signal(sem, inc=1, device_id=other, device_id_type=MESH)
        pl.semaphore_wait(sem, len(others))


class Copies:
    def __init__(self, send_sems, recv_sems):
        self.send_sems, self.recv_sems, self.used, self.started = send_sems, recv_sems, 0, []

    def start(self, src, dst, device):
        k = self.used
        self.used += 1
        copy = pltpu.make_async_remote_copy(
            src_ref=src,
            dst_ref=dst,
            send_sem=self.send_sems.at[k],
            recv_sem=self.recv_sems.at[k],
            device_id=device,
            device_id_type=MESH,
        )
        copy.start()
        self.started.append(copy)
        return copy

    def finish(self):
        for copy in self.started:
            copy.wait_send()


class RingSum:
    def __init__(self, copies, place, axis, part, r1, r2):
        self.copies, self.part, self.r1, self.r2 = copies, part, r1, r2
        self.right, self.left = place.right[axis], place.left[axis]
        pos = place.pos[axis]
        self.pos, self.rt, self.lf, self.opp = pos, (pos + 1) % 4, (pos + 3) % 4, (pos + 2) % 4

    def send_opposite(self):
        self.a = self.copies.start(self.part(self.opp, 0), self.r1.at[0], self.right)
        self.b = self.copies.start(self.part(self.opp, 1), self.r1.at[1], self.left)

    def send_right(self):
        self.d = self.copies.start(self.part(self.rt, 1), self.r2.at[0, 1], self.right)

    def send_left(self):
        self.e = self.copies.start(self.part(self.lf, 0), self.r2.at[1, 0], self.left)

    def first(self):
        self.send_opposite()
        self.send_right()
        self.send_left()

    def second(self):
        self.a.wait_recv()
        mine = self.part(self.rt, 0)
        mine[...] = (mine[...].astype(F32) + self.r1[0].astype(F32)).astype(BF16)
        self.f = self.copies.start(mine, self.r2.at[0, 0], self.right)
        self.b.wait_recv()
        mine = self.part(self.lf, 1)
        mine[...] = (mine[...].astype(F32) + self.r1[1].astype(F32)).astype(BF16)
        self.g = self.copies.start(mine, self.r2.at[1, 1], self.left)

    def total(self):
        for copy in (self.d, self.e, self.f, self.g):
            copy.wait_recv()
        return [
            self.part(self.pos, h)[...].astype(F32)
            + self.r2[0, h].astype(F32)
            + self.r2[1, h].astype(F32)
            for h in (0, 1)
        ]


class RingGather:
    def __init__(self, copies, place, axis, block):
        self.copies, self.block = copies, block
        self.right, self.left = place.right[axis], place.left[axis]
        pos = place.pos[axis]
        self.pos, self.rt, self.lf = pos, (pos + 1) % 4, (pos + 3) % 4

    def first(self):
        own = self.block(self.pos, None)
        self.a = self.copies.start(own, own, self.right)
        self.b = self.copies.start(own, own, self.left)

    def second(self):
        self.a.wait_recv()
        part = self.block(self.lf, 0)
        self.d = self.copies.start(part, part, self.right)
        self.b.wait_recv()
        part = self.block(self.rt, 1)
        self.e = self.copies.start(part, part, self.left)

    def done(self):
        self.d.wait_recv()
        self.e.wait_recv()


HALVES = ((0, 128), (128, 256))


class PlaneSum:
    def __init__(self, copies, place, terms, sums, r1a, r2a, r1b, r2b):
        x, z = place.pos["x"], place.pos["z"]
        self.sums, self.place = sums, place

        def upper(b, h):
            return terms.at[b, 2 * h : 2 * h + 2, 0:128]

        def lower(b, h):
            return terms.at[2 * h : 2 * h + 2, b, 128:256]

        self.one = (
            RingSum(copies, place, "x", upper, r1a.at[0], r2a.at[0]),
            RingSum(copies, place, "z", lower, r1a.at[1], r2a.at[1]),
        )

        def upper_two(b, h):
            return sums.at[0, b, 64 * h : 64 * h + 64]

        def lower_two(b, h):
            return sums.at[1, b, 64 * h : 64 * h + 64]

        self.two = (
            RingSum(copies, place, "z", upper_two, r1b.at[0], r2b.at[0]),
            RingSum(copies, place, "x", lower_two, r1b.at[1], r2b.at[1]),
        )

    def step1(self):
        for ring in self.one:
            ring.first()

    def step2(self):
        for ring in self.one:
            ring.second()

    def step3(self):
        for k in (0, 1):
            low, high = self.one[k].total()
            self.sums[k, 0:2] = low.astype(BF16)
            self.sums[k, 2:4] = high.astype(BF16)
            self.two[k].first()

    def step4(self):
        for ring in self.two:
            ring.second()

    def finish(self, store):
        for k in (0, 1):
            low, high = self.two[k].total()
            store(k * 128, low.astype(BF16))
            store(k * 128 + 64, high.astype(BF16))


class PlaneGather:
    def __init__(self, copies, place, buf):
        x, z = place.pos["x"], place.pos["z"]

        def upper(b, h):
            if h is None:
                return buf.at[b, z, 0:128]
            return buf.at[b, z, 64 * h : 64 * h + 64]

        def lower(b, h):
            if h is None:
                return buf.at[x, b, 128:256]
            return buf.at[x, b, 128 + 64 * h : 192 + 64 * h]

        def upper_two(b, h):
            if h is None:
                return buf.at[:, b, 0:128]
            return buf.at[2 * h : 2 * h + 2, b, 0:128]

        def lower_two(b, h):
            if h is None:
                return buf.at[b, :, 128:256]
            return buf.at[b, 2 * h : 2 * h + 2, 128:256]

        self.one = (
            RingGather(copies, place, "x", upper),
            RingGather(copies, place, "z", lower),
        )
        self.two = (
            RingGather(copies, place, "z", upper_two),
            RingGather(copies, place, "x", lower_two),
        )

    def step1(self):
        for ring in self.one:
            ring.first()

    def step2(self):
        for ring in self.one:
            ring.second()

    def step3(self):
        for one, two in zip(self.one, self.two):
            one.done()
            two.first()

    def step4(self):
        for ring in self.two:
            ring.second()

    def done(self):
        for ring in self.two:
            ring.done()


def project_kernel(
    hidden,
    encodings,
    cotangent,
    wk_hbm,
    wv_hbm,
    wq_hbm,
    wo_hbm,
    queries_out,
    grad_out,
    pair_out,
    weights,
    out_weight,
    terms,
    sums,
    r1a,
    r2a,
    r1b,
    r2b,
    pair,
    load_sems,
    send_sems,
    recv_sems,
):
    place = Place()
    copies = Copies(send_sems, recv_sems)
    loads = [
        pltpu.make_async_copy(src, weights.at[k], load_sems.at[k])
        for k, src in enumerate((wk_hbm, wv_hbm, wq_hbm))
    ]
    for load in loads:
        load.start()
    load_out = pltpu.make_async_copy(wo_hbm, out_weight, load_sems.at[3])
    place.barrier()
    left = (encodings, encodings, hidden)
    rings = [
        PlaneSum(
            copies, place, terms.at[k], sums.at[k], r1a.at[k], r2a.at[k], r1b.at[k], r2b.at[k]
        )
        for k in range(4)
    ]

    def make_terms(k):
        loads[k].wait()
        rows = left[k][...]

        def body(x, carry):
            columns = pl.ds(pl.multiple_of(x * 1024, 1024), 1024)
            product = mm(rows, weights[k, :, columns]).astype(BF16)
            for z in range(4):
                terms[k, x, z] = product[:, z * 256 : z * 256 + 256]
            return carry

        lax.fori_loop(0, 4, body, 0)

    def make_grad_terms():
        load_out.wait()
        rows = cotangent[...]

        def body(x, carry):
            for z in range(4):
                span = pl.ds(pl.multiple_of(x * 1024 + z * 256, 256), 256)
                product = lax.dot_general(rows, out_weight[span, :], NT, preferred_element_type=F32)
                terms[3, x, z] = product.astype(BF16)
            return carry

        lax.fori_loop(0, 4, body, 0)

    def pair_block(k):
        def block(b, h):
            if h is None:
                return pair.at[k, b, place.c]
            return pair.at[k, b, place.c, 128 * h : 128 * h + 128]

        return block

    gathers = [RingGather(copies, place, "y", pair_block(k)) for k in (0, 1)]

    def store_pair(k):
        def store(row, value):
            pair[k, place.y, place.c, row : row + 64] = value

        return store

    def store_queries(row, value):
        queries_out[row : row + 64] = value

    def store_grad(row, value):
        grad_out[row : row + 64] = value

    def swap(k):
        gathers[k].done()
        mine = pair.at[k, :, place.c]
        return copies.start(mine, mine, place.partner)

    keys, values, query, grad = rings
    make_terms(0)
    load_out.start()
    keys.step1()
    make_terms(1)
    values.step1()
    make_terms(2)
    keys.step2()
    query.step1()
    values.step2()
    make_grad_terms()
    keys.step3()
    values.step3()
    grad.step1()
    keys.step4()
    query.step2()
    values.step4()
    keys.finish(store_pair(0))
    gathers[0].first()
    values.finish(store_pair(1))
    gathers[1].first()
    query.step3()
    grad.step2()
    gathers[0].second()
    query.step4()
    gathers[1].second()
    grad.step3()
    swap_keys = swap(0)
    query.finish(store_queries)
    swap_values = swap(1)
    grad.step4()
    swap_keys.wait_recv()
    pair_out[0] = pair[0]
    swap_values.wait_recv()
    pair_out[1] = pair[1]
    grad.finish(store_grad)
    copies.finish()


def attend_kernel(
    nbrs, blocks, queries, grads, pair, heads_out, query_grads, dense_out, prob, dense
):
    scale = HD ** (-0.5)
    dense[...] = jnp.zeros_like(dense)
    cases = [(c, h) for c in range(4) for h in range(2)]

    def rows(ref, c, h):
        return ref[c * 64 : c * 64 + 64, h * 128 : h * 128 + 128]

    def picked(which, c, h):
        return jnp.concatenate(
            [pair[which, nbrs[c, j], :, h * 128 : h * 128 + 128] for j in (0, 1)], axis=0
        )

    slot = lax.broadcasted_iota(jnp.int32, (64, 256), 1)
    for i, (c, h) in enumerate(cases):
        limit0 = BLK * blocks[nbrs[c, 0]]
        limit1 = BLK * blocks[nbrs[c, 1]]
        valid = slot < jnp.where(slot < 128, limit0, limit1 + 128)
        scores = (
            lax.dot_general(rows(queries, c, h), picked(0, c, h), NT, preferred_element_type=F32)
            * scale
        )
        scores = jnp.where(valid, scores, -1e30)
        top = jnp.max(scores, axis=1, keepdims=True)
        terms = jnp.where(valid, jnp.exp(scores - top), 0.0)
        total = jnp.sum(terms, axis=1, keepdims=True)
        values = picked(1, c, h)
        output = mm(terms.astype(BF16), values) / total
        heads_out[c * 64 : c * 64 + 64, h * 128 : h * 128 + 128] = output.astype(BF16)
        prob[i] = terms / total
    for i, (c, h) in enumerate(cases):
        weights = prob[i]
        grad = rows(grads, c, h)
        keys = picked(0, c, h)
        value_part = lax.dot_general(weights.astype(BF16), grad, TN, preferred_element_type=F32)
        grad_prob = lax.dot_general(grad, picked(1, c, h), NT, preferred_element_type=F32)
        inner = jnp.sum(weights * grad_prob, axis=1, keepdims=True)
        grad_scores = (weights * (grad_prob - inner) * scale).astype(BF16)
        query_grads[c * 64 : c * 64 + 64, h * 128 : h * 128 + 128] = mm(grad_scores, keys).astype(
            BF16
        )
        key_part = lax.dot_general(
            grad_scores, rows(queries, c, h), TN, preferred_element_type=F32
        )
        for j in (0, 1):
            n = nbrs[c, j]
            dense[0, n, :, h * 128 : h * 128 + 128] += key_part[j * 128 : j * 128 + 128]
            dense[1, n, :, h * 128 : h * 128 + 128] += value_part[j * 128 : j * 128 + 128]
    dense_out[...] = dense[...].astype(BF16)


def finish_kernel(
    heads,
    query_grads,
    dense,
    hidden,
    encodings,
    cotangent,
    wo_hbm,
    wq_hbm,
    wk_hbm,
    wv_hbm,
    layer_out,
    grad_hidden,
    grad_encodings,
    grad_wq,
    grad_wk,
    grad_wv,
    grad_wo,
    weights,
    out_weight,
    gathered,
    theirs,
    sides,
    side_t,
    dense_in,
    dense_sum,
    dense_r1,
    dense_r2,
    parts,
    part_r1,
    part_r2,
    load_sems,
    send_sems,
    recv_sems,
):
    place = Place()
    x, y, z, c = place.x, place.y, place.z, place.c
    copies = Copies(send_sems, recv_sems)
    load_wo = pltpu.make_async_copy(wo_hbm, out_weight, load_sems.at[0])
    load_wq = pltpu.make_async_copy(wq_hbm, weights.at[1], load_sems.at[1])
    load_wk = pltpu.make_async_copy(wk_hbm, weights.at[0], load_sems.at[2])
    load_wv = pltpu.make_async_copy(wv_hbm, weights.at[1], load_sems.at[3])
    load_wo.start()
    load_wq.start()
    load_wk.start()
    gathered[0, x, z] = heads[...]
    gathered[1, x, z] = query_grads[...]
    place.barrier()
    nets = [PlaneGather(copies, place, gathered.at[k]) for k in range(4)]
    net_h, net_q, net_k, net_v = nets
    swap_dense = copies.start(dense.at[:, :, 1 - c], dense_in, place.partner)
    net_h.step1()
    net_q.step1()
    for k, ref in enumerate((cotangent, hidden, encodings)):
        sides[k, 0] = ref[...]
    swap_sides = copies.start(sides.at[:, 0], sides.at[:, 1], place.partner)

    def dense_part(b, h):
        return dense_sum.at[b, h]

    ring_dense = RingSum(copies, place, "y", dense_part, dense_r1, dense_r2)
    swap_dense.wait_recv()
    for h in (0, 1):
        for b in range(4):
            dense_sum[b, h] = (
                dense[h, b, c].astype(F32) + dense_in[h, b].astype(F32)
            ).astype(BF16)
    ring_dense.first()
    net_h.step2()
    net_q.step2()
    ring_dense.second()
    net_h.step3()
    net_q.step3()
    swap_sides.wait_recv()
    for k in range(3):
        for side in (0, 1):
            side_t[k, :, side * 256 : side * 256 + 256] = sides[k, side].T
    key_sum, value_sum = ring_dense.total()
    gathered[2, x, z] = key_sum.astype(BF16)
    gathered[3, x, z] = value_sum.astype(BF16)
    net_k.step1()
    net_v.step1()
    net_h.step4()
    net_q.step4()

    def swap_half(k):
        return copies.start(
            gathered.at[k, :, pl.ds(2 * (1 - c), 2)], theirs.at[k], place.partner
        )

    def ring_of(k):
        def part(b, h):
            return parts.at[k, b, 256 * h : 256 * h + 256]

        return RingSum(copies, place, "y", part, part_r1.at[k], part_r2.at[k])

    def weight_grad(k, side, ring):
        def block(b):
            own = jnp.concatenate([gathered[k, b, 2 * c + i] for i in (0, 1)], axis=1)
            other = jnp.concatenate([theirs[k, b, i] for i in (0, 1)], axis=1)
            both = jnp.concatenate([own, other], axis=0)
            parts[k, b] = mm(side_t[side], both).astype(BF16)

        block(ring.opp)
        ring.send_opposite()
        block(ring.rt)
        ring.send_right()
        block(ring.lf)
        ring.send_left()
        block(ring.pos)

    def wide(k, b):
        return jnp.concatenate([gathered[k, b, i] for i in range(4)], axis=1)

    def columns(b):
        return pl.ds(pl.multiple_of(b * 1024, 1024), 1024)

    def accumulate(out, make):
        out[...] = make(0)

        def body(b, carry):
            out[...] += make(b)
            return carry

        lax.fori_loop(1, 4, body, 0)

    def transposed(k, slot, b):
        return lax.dot_general(
            wide(k, b), weights[slot, :, columns(b)], NT, preferred_element_type=F32
        )

    net_h.done()
    swap_h = swap_half(0)
    load_wo.wait()
    accumulate(layer_out, lambda b: mm(wide(0, b), out_weight[columns(b), :]))
    net_k.step2()
    net_v.step2()
    rings = [ring_of(k) for k in range(4)]
    swap_h.wait_recv()
    weight_grad(0, 0, rings[0])
    net_q.done()
    swap_q = swap_half(1)
    net_k.step3()
    net_v.step3()
    load_wq.wait()
    accumulate(grad_hidden, lambda b: transposed(1, 1, b))
    load_wv.start()
    swap_q.wait_recv()
    rings[0].second()
    weight_grad(1, 1, rings[1])
    net_k.step4()
    net_v.step4()
    low, high = rings[0].total()
    grad_wo[:, 0:256] = low.T
    grad_wo[:, 256:512] = high.T
    rings[1].second()
    net_k.done()
    swap_k = swap_half(2)
    net_v.done()
    swap_v = swap_half(3)
    swap_k.wait_recv()
    weight_grad(2, 2, rings[2])
    swap_v.wait_recv()
    low, high = rings[1].total()
    grad_wq[0:256] = low
    grad_wq[256:512] = high
    rings[2].second()
    weight_grad(3, 2, rings[3])
    load_wk.wait()
    load_wv.wait()
    accumulate(grad_encodings, lambda b: transposed(2, 0, b) + transposed(3, 1, b))
    low, high = rings[2].total()
    grad_wk[0:256] = low
    grad_wk[256:512] = high
    rings[3].second()
    low, high = rings[3].total()
    grad_wv[0:256] = low
    grad_wv[256:512] = high
    copies.finish()


def vmem():
    return pl.BlockSpec(memory_space=pltpu.VMEM)


def hbm():
    return pl.BlockSpec(memory_space=pl.ANY)


def shape(*dims, dtype=BF16):
    return jax.ShapeDtypeStruct(dims, dtype)


def per_device(
    hidden,
    encodings,
    query_weight,
    key_weight,
    value_weight,
    out_weight,
    out_cotangent,
    stretch_nbrs,
    nbr_blocks,
):
    flat_enc = encodings.reshape(256, 512)
    dma = pltpu.SemaphoreType.DMA
    limit = 60 * 1024 * 1024
    queries, grads, pair = pl.pallas_call(
        project_kernel,
        out_shape=[shape(256, 256), shape(256, 256), shape(2, 4, 2, 256, 256)],
        in_specs=[vmem()] * 3 + [hbm()] * 4,
        out_specs=[vmem()] * 3,
        scratch_shapes=[
            pltpu.VMEM((3, 512, 4096), BF16),
            pltpu.VMEM((4096, 512), BF16),
            pltpu.VMEM((4, 4, 4, 256, 256), BF16),
            pltpu.VMEM((4, 2, 4, 128, 256), BF16),
            pltpu.VMEM((4, 2, 2, 2, 128, 256), BF16),
            pltpu.VMEM((4, 2, 2, 2, 2, 128, 256), BF16),
            pltpu.VMEM((4, 2, 2, 64, 256), BF16),
            pltpu.VMEM((4, 2, 2, 2, 64, 256), BF16),
            pltpu.VMEM((2, 4, 2, 256, 256), BF16),
            dma((4,)),
            dma((112,)),
            dma((112,)),
        ],
        compiler_params=pltpu.CompilerParams(
            collective_id=0, has_side_effects=True, vmem_limit_bytes=limit
        ),
    )(hidden, flat_enc, out_cotangent, key_weight, value_weight, query_weight, out_weight)
    heads, query_grads, dense = pl.pallas_call(
        attend_kernel,
        out_shape=[shape(256, 256), shape(256, 256), shape(2, 16, 128, 256)],
        in_specs=[pl.BlockSpec(memory_space=pltpu.SMEM)] * 2 + [vmem()] * 3,
        out_specs=[vmem()] * 3,
        scratch_shapes=[
            pltpu.VMEM((8, 64, 256), F32),
            pltpu.VMEM((2, 16, 128, 256), F32),
        ],
        compiler_params=pltpu.CompilerParams(vmem_limit_bytes=limit),
    )(stretch_nbrs, nbr_blocks, queries, grads, pair.reshape(2, 16, 128, 256))
    outs = pl.pallas_call(
        finish_kernel,
        out_shape=[
            shape(256, 512, dtype=F32),
            shape(256, 512, dtype=F32),
            shape(256, 512, dtype=F32),
            shape(512, 512, dtype=F32),
            shape(512, 512, dtype=F32),
            shape(512, 512, dtype=F32),
            shape(512, 512, dtype=F32),
        ],
        in_specs=[vmem()] * 6 + [hbm()] * 4,
        out_specs=[vmem()] * 7,
        scratch_shapes=[
            pltpu.VMEM((2, 512, 4096), BF16),
            pltpu.VMEM((4096, 512), BF16),
            pltpu.VMEM((4, 4, 4, 256, 256), BF16),
            pltpu.VMEM((4, 4, 2, 256, 256), BF16),
            pltpu.VMEM((3, 2, 256, 512), BF16),
            pltpu.VMEM((3, 512, 512), BF16),
            pltpu.VMEM((2, 4, 256, 256), BF16),
            pltpu.VMEM((4, 2, 256, 256), BF16),
            pltpu.VMEM((2, 256, 256), BF16),
            pltpu.VMEM((2, 2, 256, 256), BF16),
            pltpu.VMEM((4, 4, 512, 512), BF16),
            pltpu.VMEM((4, 2, 256, 512), BF16),
            pltpu.VMEM((4, 2, 2, 256, 512), BF16),
            dma((4,)),
            dma((112,)),
            dma((112,)),
        ],
        compiler_params=pltpu.CompilerParams(
            collective_id=1, has_side_effects=True, vmem_limit_bytes=limit
        ),
    )(
        heads,
        query_grads,
        dense.reshape(2, 4, 2, 256, 256),
        hidden,
        flat_enc,
        out_cotangent,
        out_weight,
        query_weight,
        key_weight,
        value_weight,
    )
    layer_out, grad_hidden, grad_enc, grad_wq, grad_wk, grad_wv, grad_wo = outs
    return (
        layer_out,
        grad_hidden,
        grad_enc.reshape(encodings.shape),
        grad_wq,
        grad_wk,
        grad_wv,
        grad_wo,
    )


def solution(mesh):
    in_specs = (
        P("dp", "enc"),
        P("dp", None, "enc"),
        P("enc", None),
        P("enc", None),
        P("enc", None),
        P(None, "enc"),
        P("dp", "enc"),
        P("dp", None),
        P(),
    )
    out_specs = (
        P("dp", "enc"),
        P("dp", "enc"),
        P("dp", None, "enc"),
        P("enc", "dp"),
        P("enc", "dp"),
        P("enc", "dp"),
        P("dp", "enc"),
    )
    return jax.shard_map(
        per_device, mesh=mesh, in_specs=in_specs, out_specs=out_specs, check_vma=False
    )
```

time: 647 us -> 195 us (0.30)
  waiting for transfers between devices: 538 us -> 0 us
  Pallas kernels: 0 us -> 181 us
  matrix products: 45.4 us -> 0 us
  other arithmetic: 21.8 us -> 0 us
  local copies, waits for them, and re-layouts: 26.2 us -> 12.4 us
  between operations: 14.3 us -> 0.67 us
    reduce_scatter x7 -> x0, waiting for transfers between devices: 366 us -> none  [the longest x1 79.8 us: per_device(): lax.psum_scatter(grad_part, 'enc', scatter_dimension=1, tiled=True)]
    pallas_call x0 -> x3, Pallas kernels: none -> 181 us  [the longest x1 109 us: per_device(): pl.pallas_call(finish_kernel, out_shape=[shape(256, 512, dtype=F32), shap...]
    all_gather x4 -> x0, waiting for transfers between devices: 172 us -> none  [the longest x1 54.5 us: per_device(): all_pair_grads = lax.all_gather(home_sums, 'enc', axis=3, tiled=True)]
    dot_general x19 -> x0, matrix products: 45.4 us -> none  [the longest x1 5.4 us: per_device(): lax.dot_general(out_cotangent, out_weight, (((1,), (1,)), ((), ())), pref...]
    another operation x2 -> x0, other arithmetic: 9.97 us -> none  [the longest x1 6.19 us: per_device(): jnp.stack([lax.dot_general(flat_enc, flat_grads[0], (((0,), (0,)), ((), (...]
    convert_element_type x7 -> x0, other arithmetic: 8.67 us -> none  [the longest x1 2.14 us: per_device(): grad_out_weight = lax.psum_scatter(lax.dot_general(all_heads, out_cotange...]
  transfers between devices with their start and end apart: 11 -> 0, of which waited for: 11 -> 0; matrix products, arithmetic and copies ran while one was open for 9% -> 0% of each run, Pallas kernels for 0% -> 0%
where the time goes in v1:
time: 195 us; the launch traced here: 194 us
  Pallas kernels  181 us (93%)
  local copies, waits for them, and re-layouts  12.4 us (6%)
    pallas_call x1, Pallas kernels, per_device(): pl.pallas_call(finish_kernel, out_shape=[shape(256, 512, dtype=F32), shap...  109 us
    pallas_call x1, Pallas kernels, per_device(): pl.pallas_call(project_kernel, out_shape=[shape(256, 256), shape(256, 256...  64.9 us
    unnamed x14, local copies, waits for them, and re-layouts  12.4 us
    pallas_call x1, Pallas kernels, per_device(): pl.pallas_call(attend_kernel, out_shape=[shape(256, 256), shape(256, 256)...  7.75 us

profile of v1, /device:TPU:0, one launch (start us, length us, event | category | flops | bytes accessed | tf_op | source)
XLA Modules:
  0.0 194.4 jit_solution(11246998178392519203)
XLA Ops:
  0.6 1.3 copy.16.nbrs
  2.0 64.9 %shard_map.144 = (bf16[256,256]{1,0:T(8,128)(2,1)}, bf16[256,256]{1,0:T(8,128)(2,1)}, bf16[2,4,2,256,256]{4,3,2,1,0:T(8,128)(2,1)}) custom-call(bf16[256,512]{1,0:T(8,128)(2,1)} %hidden.3, bf16[256,512]{1,0:T(8,128)(2,1)} %bitcast.6, bf16[256,512]{1,0:T(8,128)(2,1)} %cotangent.3, bf16[512,4096]{1,0:T(8,128)(2,1)} %wk_hbm.3, bf16[512,4096]{1,0:T(8,128)(2,1)} %wv_hbm.3, ...), custom_call_target="tpu_custom_call" | custom-call | tf_op jit(solution)/shard_map/pallas_call | solution.py:649
  66.9 7.8 %shard_map.145 = (bf16[256,256]{1,0:T(8,128)(2,1)}, bf16[256,256]{1,0:T(8,128)(2,1)}, bf16[2,16,128,256]{3,2,1,0:T(8,128)(2,1)}) custom-call(s32[4,2]{1,0:T(4,128)} %copy.16.nbrs, s32[16]{0:T(128)} %blocks.1, bf16[256,256]{1,0:T(8,128)(2,1)} %get-tuple-element.20.queries, bf16[256,256]{1,0:T(8,128)(2,1)} %get-tuple-element.21.grads, ...), custom_call_target="tpu_custom_call" | custom-call | tf_op jit(solution)/shard_map/pallas_call | solution.py:672
  74.7 108.6 %shard_map.146 = (f32[256,512]{1,0:T(8,128)}, f32[256,512]{1,0:T(8,128)}, f32[256,512]{1,0:T(8,128)}, f32[512,512]{1,0:T(8,128)}, f32[512,512]{1,0:T(8,128)}, /*index=5*/f32[512,512]{1,0:T(8,128)}, f32[512,512]{1,0:T(8,128)}) custom-call(bf16[256,256]{1,0:T(8,128)(2,1)} %get-tuple-element.23.heads, bf16[256,256]{1,0:T(8,128)(2,1)} %get-tuple-element.24.query_grads, ...), custom_call_target="tpu_custom_call" | custom-call | tf_op jit(solution)/shard_map/pallas_call | solution.py:683
  183.3 0.0 copy-start.2
  183.3 0.0 copy-start.1
  183.3 2.0 %copy.24 = f32[256,512]{1,0:T(8,128)} copy(f32[256,512]{1,0:T(8,128)} %get-tuple-element.40) | data formatting | bytes 1048576
  185.4 0.0 copy-start
  185.4 2.0 %copy.25 = f32[256,512]{1,0:T(8,128)} copy(f32[256,512]{1,0:T(8,128)} %get-tuple-element.41) | data formatting | bytes 1048576
  187.3 1.9 copy.26
  189.2 2.3 %copy.27 = f32[512,512]{1,0:T(8,128)} copy(f32[512,512]{1,0:T(8,128)} %get-tuple-element.43) | data formatting | bytes 2097152
  191.4 0.0 copy-done.2
  191.5 1.0 copy.28
  192.4 0.0 copy-done.1
  192.4 1.0 copy.29
  193.4 0.0 copy-done
  193.4 1.0 copy.30
Async XLA Ops:
  183.3 8.1 %copy-start.2 = (f32[512,512]{1,0:T(8,128)S(1)}, f32[512,512]{1,0:T(8,128)}, u32[]{:S(2)}) copy-start(f32[512,512]{1,0:T(8,128)} %get-tuple-element.44) | copy-start | bytes 3145732
  183.3 9.1 %copy-start.1 = (f32[512,512]{1,0:T(8,128)S(1)}, f32[512,512]{1,0:T(8,128)}, u32[]{:S(2)}) copy-start(f32[512,512]{1,0:T(8,128)} %get-tuple-element.45) | copy-start | bytes 3145732
  185.4 8.0 %copy-start = (f32[512,512]{1,0:T(8,128)S(1)}, f32[512,512]{1,0:T(8,128)}, u32[]{:S(2)}) copy-start(f32[512,512]{1,0:T(8,128)} %get-tuple-element.46) | copy-start | bytes 3145732

commit v2 on v1

v2 whole, which is shorter than its diff:
```python
import functools

import jax
import jax.numpy as jnp
from jax import lax
from jax.experimental import pallas as pl
from jax.experimental.pallas import tpu as pltpu
from jax.sharding import PartitionSpec as P

HD = 128
BLK = 16
MESH = pl.DeviceIdType.MESH
F32 = jnp.float32
BF16 = jnp.bfloat16
NT = (((1,), (1,)), ((), ()))
TN = (((0,), (0,)), ((), ()))


def mm(a, b):
    return jnp.dot(a, b, preferred_element_type=F32)


class Place:
    def __init__(self):
        self.dp = lax.axis_index("dp")
        self.enc = lax.axis_index("enc")
        dp, enc = self.dp, self.enc
        self.y, self.c = dp // 2, dp % 2
        self.x, self.z = enc // 4, enc % 4
        x, y, z, c = self.x, self.y, self.z, self.c
        self.right = {
            "x": (dp, ((x + 1) % 4) * 4 + z),
            "z": (dp, x * 4 + (z + 1) % 4),
            "y": (((y + 1) % 4) * 2 + c, enc),
        }
        self.left = {
            "x": (dp, ((x + 3) % 4) * 4 + z),
            "z": (dp, x * 4 + (z + 3) % 4),
            "y": (((y + 3) % 4) * 2 + c, enc),
        }
        self.pos = {"x": x, "y": y, "z": z}
        self.partner = (y * 2 + (1 - c), enc)
        self.near = list(self.right.values()) + list(self.left.values()) + [self.partner]

    def column(self):
        steps = [(0, 1), (1, 0), (3, 0), (1, 1), (3, 1), (2, 0), (2, 1)]
        return [((self.y + dy) % 4, 1 - self.c if dc else self.c) for dy, dc in steps]

    def greet(self, others):
        sem = pltpu.get_barrier_semaphore()
        for other in others:
            pl.semaphore_signal(sem, inc=1, device_id=other, device_id_type=MESH)

    def meet(self, others):
        pl.semaphore_wait(pltpu.get_barrier_semaphore(), len(others))


class Copies:
    def __init__(self, send_sems, recv_sems):
        self.send_sems, self.recv_sems, self.used, self.started = send_sems, recv_sems, 0, []

    def start(self, src, dst, device):
        k = self.used
        self.used += 1
        copy = pltpu.make_async_remote_copy(
            src_ref=src,
            dst_ref=dst,
            send_sem=self.send_sems.at[k],
            recv_sem=self.recv_sems.at[k],
            device_id=device,
            device_id_type=MESH,
        )
        copy.start()
        self.started.append(copy)
        return copy

    def flush(self, some):
        for copy in some:
            copy.wait_send()
        gone = [id(copy) for copy in some]
        self.started = [copy for copy in self.started if id(copy) not in gone]

    def finish(self):
        self.flush(list(self.started))


class RingSum:
    def __init__(self, copies, place, axis, part, r1, r2):
        self.copies, self.part, self.r1, self.r2 = copies, part, r1, r2
        self.right, self.left = place.right[axis], place.left[axis]
        pos = place.pos[axis]
        self.pos, self.rt, self.lf, self.opp = pos, (pos + 1) % 4, (pos + 3) % 4, (pos + 2) % 4

    def send_opposite(self):
        self.a = self.copies.start(self.part(self.opp, 0), self.r1.at[0], self.right)
        self.b = self.copies.start(self.part(self.opp, 1), self.r1.at[1], self.left)

    def send_right(self):
        self.d = self.copies.start(self.part(self.rt, 1), self.r2.at[0, 1], self.right)

    def send_left(self):
        self.e = self.copies.start(self.part(self.lf, 0), self.r2.at[1, 0], self.left)

    def first(self):
        self.send_opposite()
        self.send_right()
        self.send_left()

    def second(self):
        self.a.wait_recv()
        mine = self.part(self.rt, 0)
        mine[...] = (mine[...].astype(F32) + self.r1[0].astype(F32)).astype(BF16)
        self.f = self.copies.start(mine, self.r2.at[0, 0], self.right)
        self.b.wait_recv()
        mine = self.part(self.lf, 1)
        mine[...] = (mine[...].astype(F32) + self.r1[1].astype(F32)).astype(BF16)
        self.g = self.copies.start(mine, self.r2.at[1, 1], self.left)

    def flush(self):
        self.copies.flush([self.a, self.b, self.d, self.e, self.f, self.g])

    def total(self):
        for copy in (self.d, self.e, self.f, self.g):
            copy.wait_recv()
        return [
            self.part(self.pos, h)[...].astype(F32)
            + self.r2[0, h].astype(F32)
            + self.r2[1, h].astype(F32)
            for h in (0, 1)
        ]


class RingGather:
    def __init__(self, copies, place, axis, block):
        self.copies, self.block = copies, block
        self.right, self.left = place.right[axis], place.left[axis]
        pos = place.pos[axis]
        self.pos, self.rt, self.lf = pos, (pos + 1) % 4, (pos + 3) % 4

    def first(self):
        own = self.block(self.pos, None)
        self.a = self.copies.start(own, own, self.right)
        self.b = self.copies.start(own, own, self.left)

    def second(self):
        self.a.wait_recv()
        part = self.block(self.lf, 0)
        self.d = self.copies.start(part, part, self.right)
        self.b.wait_recv()
        part = self.block(self.rt, 1)
        self.e = self.copies.start(part, part, self.left)

    def done(self):
        self.d.wait_recv()
        self.e.wait_recv()

    def flush(self):
        self.copies.flush([self.a, self.b, self.d, self.e])


HALVES = ((0, 128), (128, 256))


class PlaneSum:
    def __init__(self, copies, place, terms, sums, r1a, r2a, r1b, r2b):
        x, z = place.pos["x"], place.pos["z"]
        self.sums, self.place = sums, place

        def upper(b, h):
            return terms.at[b, 2 * h : 2 * h + 2, 0:128]

        def lower(b, h):
            return terms.at[2 * h : 2 * h + 2, b, 128:256]

        self.one = (
            RingSum(copies, place, "x", upper, r1a.at[0], r2a.at[0]),
            RingSum(copies, place, "z", lower, r1a.at[1], r2a.at[1]),
        )

        def upper_two(b, h):
            return sums.at[0, b, 64 * h : 64 * h + 64]

        def lower_two(b, h):
            return sums.at[1, b, 64 * h : 64 * h + 64]

        self.two = (
            RingSum(copies, place, "z", upper_two, r1b.at[0], r2b.at[0]),
            RingSum(copies, place, "x", lower_two, r1b.at[1], r2b.at[1]),
        )

    def step1(self):
        for ring in self.one:
            ring.first()

    def step2(self):
        for ring in self.one:
            ring.second()

    def step3(self):
        for k in (0, 1):
            low, high = self.one[k].total()
            self.sums[k, 0:2] = low.astype(BF16)
            self.sums[k, 2:4] = high.astype(BF16)
            self.two[k].first()

    def step4(self):
        for ring in self.one:
            ring.flush()
        for ring in self.two:
            ring.second()

    def finish(self, store):
        for k in (0, 1):
            low, high = self.two[k].total()
            store(k * 128, low.astype(BF16))
            store(k * 128 + 64, high.astype(BF16))


class PlaneGather:
    def __init__(self, copies, place, buf):
        x, z = place.pos["x"], place.pos["z"]
        half = buf.shape[2] // 2
        quarter = half // 2

        def upper(b, h):
            if h is None:
                return buf.at[b, z, 0:half]
            return buf.at[b, z, quarter * h : quarter * h + quarter]

        def lower(b, h):
            if h is None:
                return buf.at[x, b, half : 2 * half]
            return buf.at[x, b, half + quarter * h : half + quarter * h + quarter]

        def upper_two(b, h):
            if h is None:
                return buf.at[:, b, 0:half]
            return buf.at[2 * h : 2 * h + 2, b, 0:half]

        def lower_two(b, h):
            if h is None:
                return buf.at[b, :, half : 2 * half]
            return buf.at[b, 2 * h : 2 * h + 2, half : 2 * half]

        self.one = (
            RingGather(copies, place, "x", upper),
            RingGather(copies, place, "z", lower),
        )
        self.two = (
            RingGather(copies, place, "z", upper_two),
            RingGather(copies, place, "x", lower_two),
        )

    def step1(self):
        for ring in self.one:
            ring.first()

    def step2(self):
        for ring in self.one:
            ring.second()

    def step3(self):
        for one, two in zip(self.one, self.two):
            one.done()
            two.first()

    def step4(self):
        for ring in self.two:
            ring.second()

    def done(self):
        for ring in self.two:
            ring.done()


def layer_kernel(
    nbrs,
    blocks,
    hidden,
    encodings,
    cotangent,
    wk_hbm,
    wv_hbm,
    wq_hbm,
    wo_hbm,
    layer_hbm,
    grad_hidden_hbm,
    grad_encodings_hbm,
    grad_wq_hbm,
    grad_wk_hbm,
    grad_wv_hbm,
    grad_wo_hbm,
    weights,
    out_weight,
    terms,
    sums,
    r1a,
    r2a,
    r1b,
    r2b,
    pair,
    cots,
    encs,
    hids,
    queries,
    grads,
    prob,
    scored,
    flipped,
    spread_h,
    spread_v,
    theirs,
    side_t,
    dense_in,
    dense_sum,
    dense_r,
    part_r1,
    part_r2,
    rows_out,
    grads_out,
    load_sems,
    send_sems,
    recv_sems,
):
    place = Place()
    x, y, z, c = place.x, place.y, place.z, place.c
    copies = Copies(send_sems, recv_sems)
    column = place.column()
    met = place.near + [(oy * 2 + oc, place.enc) for oy, oc in column[3:]]
    loads = [
        pltpu.make_async_copy(src, dst, load_sems.at[k])
        for k, (src, dst) in enumerate(
            [
                (wk_hbm, weights.at[0]),
                (wv_hbm, weights.at[1]),
                (wq_hbm, weights.at[2]),
                (wo_hbm, out_weight),
            ]
        )
    ]
    for load in loads:
        load.start()
    place.greet(met)
    results = [
        pltpu.make_async_copy(src, dst, load_sems.at[4 + k])
        for k, (src, dst) in enumerate(
            [
                (rows_out.at[0], layer_hbm),
                (rows_out.at[1], grad_hidden_hbm),
                (rows_out.at[2], grad_encodings_hbm),
                (grads_out.at[0], grad_wq_hbm),
                (grads_out.at[0], grad_wk_hbm),
                (grads_out.at[1], grad_wv_hbm),
                (grads_out.at[1], grad_wo_hbm),
            ]
        )
    ]

    left = (encodings, encodings, hidden)
    keys, values, query, grad = [
        PlaneSum(
            copies, place, terms.at[k], sums.at[k], r1a.at[k], r2a.at[k], r1b.at[k], r2b.at[k]
        )
        for k in range(4)
    ]

    def make_terms(k):
        loads[k].wait()
        rows = left[k][...]

        def body(b, carry):
            product = mm(rows, weights[k, :, columns(b)]).astype(BF16)
            for i in range(4):
                terms[k, b, i] = product[:, i * 256 : i * 256 + 256]
            return carry

        lax.fori_loop(0, 4, body, 0)

    def make_grad_terms():
        loads[3].wait()
        rows = cotangent[...]

        def body(b, carry):
            for i in range(4):
                span = pl.ds(pl.multiple_of(b * 1024 + i * 256, 256), 256)
                product = lax.dot_general(rows, out_weight[span, :], NT, preferred_element_type=F32)
                terms[3, b, i] = product.astype(BF16)
            return carry

        lax.fori_loop(0, 4, body, 0)

    def columns(b):
        return pl.ds(pl.multiple_of(b * 1024, 1024), 1024)

    def row_block(ref):
        def block(b, h):
            if h is None:
                return ref.at[b, c]
            return ref.at[b, c, 128 * h : 128 * h + 128]

        return block

    def pair_block(k):
        def block(b, h):
            if h is None:
                return pair.at[k, b, c]
            return pair.at[k, b, c, h]

        return block

    gather_cots = RingGather(copies, place, "y", row_block(cots))
    gather_encs = RingGather(copies, place, "y", row_block(encs))
    gather_keys, gather_values = [
        RingGather(copies, place, "y", pair_block(k)) for k in (0, 1)
    ]

    def swap(gather, mine):
        gather.done()
        return copies.start(mine, mine, place.partner)

    def store_pair(k):
        def store(row, value):
            at = row % 128
            pair[k, y, c, row // 128, at : at + 64] = value

        return store

    def store_to(ref):
        def store(row, value):
            ref[row : row + 64] = value

        return store

    scale = HD ** (-0.5)
    cases = [(t, h) for t in range(4) for h in range(2)]

    def rows_of(ref, t, h):
        return ref[t * 64 : t * 64 + 64, h * 128 : h * 128 + 128]

    def picked(which, t, h):
        return jnp.concatenate(
            [
                pair[which, n // 4, (n // 2) % 2, n % 2, :, h * 128 : h * 128 + 128]
                for n in (nbrs[t, 0], nbrs[t, 1])
            ],
            axis=0,
        )

    def attend():
        slot = lax.broadcasted_iota(jnp.int32, (64, 256), 1)
        for i, (t, h) in enumerate(cases):
            limit0 = BLK * blocks[nbrs[t, 0]]
            limit1 = BLK * blocks[nbrs[t, 1]]
            valid = slot < jnp.where(slot < 128, limit0, limit1 + 128)
            scores = (
                lax.dot_general(
                    rows_of(queries, t, h), picked(0, t, h), NT, preferred_element_type=F32
                )
                * scale
            )
            scores = jnp.where(valid, scores, -1e30)
            top = jnp.max(scores, axis=1, keepdims=True)
            exps = jnp.where(valid, jnp.exp(scores - top), 0.0)
            total = jnp.sum(exps, axis=1, keepdims=True)
            output = mm(exps.astype(BF16), picked(1, t, h)) / total
            terms[0, x, z, t * 64 : t * 64 + 64, h * 128 : h * 128 + 128] = output.astype(BF16)
            prob[h, t * 64 : t * 64 + 64] = exps / total

    def attend_back():
        for t, h in cases:
            weight = prob[h, t * 64 : t * 64 + 64]
            grad_prob = lax.dot_general(
                rows_of(grads, t, h), picked(1, t, h), NT, preferred_element_type=F32
            )
            inner = jnp.sum(weight * grad_prob, axis=1, keepdims=True)
            found = weight * (grad_prob - inner) * scale
            scored[h, t * 64 : t * 64 + 64] = found
            term = mm(found.astype(BF16), picked(0, t, h))
            terms[1, x, z, t * 64 : t * 64 + 64, h * 128 : h * 128 + 128] = term.astype(BF16)

    def flip(source):
        for h in range(2):
            flipped[h] = source[h].T

    def neighbour_grads(which, rows):
        lane = lax.broadcasted_iota(jnp.int32, (128, 256), 1)
        names = []
        for j in range(2):
            name = jnp.where(lane < 64, nbrs[0, j], nbrs[1, j])
            name = jnp.where(lane < 128, name, nbrs[2, j])
            names.append(jnp.where(lane < 192, name, nbrs[3, j]))

        def body(i, carry):
            for h in range(2):
                first, second = flipped[h, 0:128], flipped[h, 128:256]
                chosen = jnp.concatenate(
                    [
                        jnp.where(
                            names[0] == n,
                            first,
                            jnp.where(names[1] == n, second, jnp.zeros_like(first)),
                        )
                        for n in (2 * i, 2 * i + 1)
                    ],
                    axis=0,
                ).astype(BF16)
                term = mm(chosen, rows[:, h * 128 : h * 128 + 128]).astype(BF16)
                for j in range(2):
                    pair[which, i // 2, i % 2, j, :, h * 128 : h * 128 + 128] = term[
                        j * 128 : j * 128 + 128
                    ]
            return carry

        lax.fori_loop(0, 8, body, 0)

    def swap_dense(k):
        return copies.start(pair.at[k, :, 1 - c], dense_in.at[k], place.partner)

    def send_dense(k, swapped):
        swapped.wait_recv()
        for b in range(4):
            dense_sum[b, k] = (pair[k, b, c].astype(F32) + dense_in[k, b].astype(F32)).astype(BF16)
        return [
            copies.start(
                dense_sum.at[(y + step) % 4, k],
                dense_r.at[i, k],
                (((y + step) % 4) * 2 + c, place.enc),
            )
            for i, step in enumerate((1, 3, 2))
        ]

    def sum_dense(k, moves):
        for move in moves:
            move.wait_recv()
        total = dense_sum[y, k].astype(F32)
        for i in range(3):
            total = total + dense_r[i, k].astype(F32)
        terms[2 + k, x, z] = total.astype(BF16).reshape(256, 256)

    net_h, net_q, net_k, net_v = [PlaneGather(copies, place, terms.at[k]) for k in range(4)]
    net_sh, net_sv = [PlaneGather(copies, place, ref) for ref in (spread_h, spread_v)]

    def swap_half(k):
        return copies.start(terms.at[k, :, pl.ds(2 * (1 - c), 2)], theirs.at[k - 1], place.partner)

    def ring_of(k):
        def part(b, h):
            return r2a.at[2 * (k - 1) + b // 2, b % 2, h]

        return RingSum(copies, place, "y", part, part_r1.at[k - 1], part_r2.at[k - 1])

    def weight_grad(k, ring):
        def block(b):
            own = jnp.concatenate([terms[k, b, 2 * c + i] for i in (0, 1)], axis=1)
            other = jnp.concatenate([theirs[k - 1, b, i] for i in (0, 1)], axis=1)
            both = jnp.concatenate([own, other], axis=0)
            product = mm(side_t[k - 1], both).astype(BF16)
            for h in (0, 1):
                for i in (0, 1):
                    quarter = product[256 * h : 256 * h + 256, 256 * i : 256 * i + 256]
                    r2a[2 * (k - 1) + b // 2, b % 2, h, i] = quarter.reshape(2, 128, 256)

        block(ring.opp)
        ring.send_opposite()
        block(ring.rt)
        ring.send_right()
        block(ring.lf)
        ring.send_left()
        block(ring.pos)

    def store_grad(k, ring):
        for h, found in enumerate(ring.total()):
            for i in (0, 1):
                grads_out[0, 256 * h : 256 * h + 256, 256 * i : 256 * i + 256] = found[i].reshape(
                    256, 256
                )
        results[2 + k].start()

    def wide(k, b):
        return jnp.concatenate([terms[k, b, i] for i in range(4)], axis=1)

    def accumulate(k, make):
        rows_out[k] = make(0)

        def body(b, carry):
            rows_out[k] += make(b)
            return carry

        lax.fori_loop(1, 4, body, 0)
        results[k].start()

    def transposed(k, slot, b):
        return lax.dot_general(
            wide(k, b), weights[slot, :, columns(b)], NT, preferred_element_type=F32
        )

    def turn(source, store):
        def body(t, carry):
            rows = []
            for e in (2 * t, 2 * t + 1):
                span = pl.ds(pl.multiple_of(e * 16, 16), 16)
                rows += [source[d // 2, d % 2, span] for d in range(8)]
            store(t, jnp.concatenate(rows, axis=0).T)
            return carry

        lax.fori_loop(0, 8, body, 0)

    def store_cots(t, found):
        for i in range(4):
            sums[t // 2, t % 2, i] = found[128 * i : 128 * i + 128]

    def store_encs(t, found):
        for i in range(4):
            r1a[t // 2, t % 2, i // 2, i % 2] = found[128 * i : 128 * i + 128]

    def exchange(k, spread):
        span = pl.ds(pl.multiple_of(place.enc * 16, 16), 16)
        moves = [
            copies.start(
                terms.at[k, oy, pl.ds(2 * oc, 2), span],
                spread.at[x, z, place.dp],
                (oy * 2 + oc, place.enc),
            )
            for oy, oc in column
        ]
        spread[x, z, place.dp] = terms[k, y, pl.ds(2 * c, 2), span]
        return moves

    def whole_grad(turned, spread):
        total = None
        for b in range(4):
            sides = jnp.concatenate(
                [
                    jnp.concatenate([turned(b, j, i) for j in (0, 1)], axis=1) for i in range(4)
                ],
                axis=0,
            )
            rows = jnp.concatenate(
                [
                    jnp.concatenate([spread[b, k, :, i].reshape(128, 256) for i in (0, 1)], axis=1)
                    for k in range(4)
                ],
                axis=0,
            )
            term = mm(sides, rows)
            total = term if total is None else total + term
        return total

    cots[y, c] = cotangent[...]
    encs[y, c] = encodings[...]
    hids[0] = hidden[...]
    make_terms(0)
    place.meet(met)
    keys.step1()
    gather_cots.first()
    swap_hids = copies.start(hids.at[0], hids.at[1], place.partner)
    make_terms(1)
    values.step1()
    gather_encs.first()
    make_terms(2)
    keys.step2()
    query.step1()
    values.step2()
    gather_cots.second()
    make_grad_terms()
    keys.step3()
    values.step3()
    grad.step1()
    keys.step4()
    gather_encs.second()
    query.step2()
    values.step4()
    keys.finish(store_pair(0))
    gather_keys.first()
    values.finish(store_pair(1))
    gather_values.first()
    swap_cots = swap(gather_cots, cots.at[:, c])
    swap_encs = swap(gather_encs, encs.at[:, c])
    query.step3()
    grad.step2()
    gather_keys.second()
    query.step4()
    gather_values.second()
    grad.step3()
    swap_keys = swap(gather_keys, pair.at[0, :, c])
    query.finish(store_to(queries))
    swap_values = swap(gather_values, pair.at[1, :, c])
    swap_keys.wait_recv()
    swap_values.wait_recv()
    attend()
    net_h.step1()
    grad.step4()
    flip(prob)
    net_h.step2()
    grad.finish(store_to(grads))
    attend_back()
    net_q.step1()
    net_h.step3()
    gather_keys.flush()
    gather_values.flush()
    copies.flush([swap_keys, swap_values])
    neighbour_grads(1, grads)
    swap_dense_v = swap_dense(1)
    flip(scored)
    neighbour_grads(0, queries)
    swap_dense_k = swap_dense(0)
    net_q.step2()
    moves_dv = send_dense(1, swap_dense_v)
    moves_dk = send_dense(0, swap_dense_k)
    net_q.step3()
    swap_hids.wait_recv()
    for k in (0, 1):
        side_t[0, :, k * 256 : k * 256 + 256] = hids[k].T
    net_h.step4()
    sum_dense(1, moves_dv)
    net_v.step1()
    sum_dense(0, moves_dk)
    net_k.step1()
    net_q.step4()
    net_v.step2()
    net_k.step2()
    net_h.done()
    moves_h = exchange(0, spread_h)
    net_v.step3()
    net_q.done()
    swap_q = swap_half(1)
    net_k.step3()
    ring_q, ring_k = ring_of(1), ring_of(2)
    swap_q.wait_recv()
    weight_grad(1, ring_q)
    for move in moves_h:
        move.wait_recv()
    net_sh.step1()
    swap_encs.wait_recv()
    side_t[1, :, 0:256] = encs[y, c].T
    side_t[1, :, 256:512] = encs[y, 1 - c].T
    net_v.step4()
    net_k.step4()
    net_sh.step2()
    accumulate(0, lambda b: mm(wide(0, b), out_weight[columns(b), :]))
    net_v.done()
    moves_v = exchange(3, spread_v)
    net_k.done()
    swap_k = swap_half(2)
    ring_q.second()
    for move in moves_v:
        move.wait_recv()
    net_sv.step1()
    net_sh.step3()
    swap_k.wait_recv()
    weight_grad(2, ring_k)
    net_sv.step2()
    swap_cots.wait_recv()
    for total in (keys, values, query, grad):
        for ring in total.two:
            ring.flush()
    turn(cots, store_cots)
    net_sv.step3()
    accumulate(1, lambda b: transposed(1, 2, b))
    net_sh.step4()
    turn(encs, store_encs)
    store_grad(1, ring_q)
    accumulate(2, lambda b: transposed(2, 0, b) + transposed(3, 1, b))
    net_sv.step4()
    net_sh.done()
    grads_out[1] = whole_grad(lambda b, j, i: sums[b, j, i], spread_h).T
    results[6].start()
    ring_k.second()
    net_sv.done()
    results[6].wait()
    grads_out[1] = whole_grad(lambda b, j, i: r1a[b, j, i // 2, i % 2], spread_v)
    results[5].start()
    results[3].wait()
    store_grad(2, ring_k)
    for k in (0, 1, 2, 4, 5):
        results[k].wait()
    copies.finish()


def copy_kernel(*refs):
    sems = refs[-1]
    count = (len(refs) - 1) // 3
    loads, moves = [], []
    for k in range(count):
        held = refs[2 * count + k]
        loads.append(pltpu.make_async_copy(refs[k], held, sems.at[0, k]))
        moves.append(pltpu.make_async_copy(held, refs[count + k], sems.at[1, k]))
    for load in loads:
        load.start()
    for load, move in zip(loads, moves):
        load.wait()
        move.start()
    for move in moves:
        move.wait()


def vmem():
    return pl.BlockSpec(memory_space=pltpu.VMEM)


def hbm():
    return pl.BlockSpec(memory_space=pl.ANY)


def shape(*dims, dtype=BF16):
    return jax.ShapeDtypeStruct(dims, dtype)


def per_device(
    hidden,
    encodings,
    query_weight,
    key_weight,
    value_weight,
    out_weight,
    out_cotangent,
    stretch_nbrs,
    nbr_blocks,
):
    flat_enc = encodings.reshape(256, 512)
    dma = pltpu.SemaphoreType.DMA
    limit = 62 * 1024 * 1024
    results = [shape(256, 512, dtype=F32)] * 3 + [shape(512, 512, dtype=F32)] * 4
    outs = pl.pallas_call(
        layer_kernel,
        out_shape=results,
        in_specs=[pl.BlockSpec(memory_space=pltpu.SMEM)] * 2 + [vmem()] * 3 + [hbm()] * 4,
        out_specs=[hbm()] * 7,
        scratch_shapes=[
            pltpu.VMEM((3, 512, 4096), BF16),
            pltpu.VMEM((4096, 512), BF16),
            pltpu.VMEM((4, 4, 4, 256, 256), BF16),
            pltpu.VMEM((4, 2, 4, 128, 256), BF16),
            pltpu.VMEM((4, 2, 2, 2, 128, 256), BF16),
            pltpu.VMEM((4, 2, 2, 2, 2, 128, 256), BF16),
            pltpu.VMEM((4, 2, 2, 64, 256), BF16),
            pltpu.VMEM((4, 2, 2, 2, 64, 256), BF16),
            pltpu.VMEM((2, 4, 2, 2, 128, 256), BF16),
            pltpu.VMEM((4, 2, 256, 512), BF16),
            pltpu.VMEM((4, 2, 256, 512), BF16),
            pltpu.VMEM((2, 256, 512), BF16),
            pltpu.VMEM((256, 256), BF16),
            pltpu.VMEM((256, 256), BF16),
            pltpu.VMEM((2, 256, 256), F32),
            pltpu.VMEM((2, 256, 256), F32),
            pltpu.VMEM((2, 256, 256), F32),
            pltpu.VMEM((4, 4, 8, 2, 16, 256), BF16),
            pltpu.VMEM((4, 4, 8, 2, 16, 256), BF16),
            pltpu.VMEM((2, 4, 2, 256, 256), BF16),
            pltpu.VMEM((2, 512, 512), BF16),
            pltpu.VMEM((2, 4, 2, 128, 256), BF16),
            pltpu.VMEM((4, 2, 2, 128, 256), BF16),
            pltpu.VMEM((3, 2, 2, 128, 256), BF16),
            pltpu.VMEM((2, 2, 2, 2, 128, 256), BF16),
            pltpu.VMEM((2, 2, 2, 2, 2, 128, 256), BF16),
            pltpu.VMEM((3, 256, 512), F32),
            pltpu.VMEM((2, 512, 512), F32),
            dma((11,)),
            dma((256,)),
            dma((256,)),
        ],
        compiler_params=pltpu.CompilerParams(
            collective_id=0, has_side_effects=True, vmem_limit_bytes=limit
        ),
    )(
        stretch_nbrs,
        nbr_blocks,
        hidden,
        flat_enc,
        out_cotangent,
        key_weight,
        value_weight,
        query_weight,
        out_weight,
    )
    outs = pl.pallas_call(
        copy_kernel,
        out_shape=results,
        in_specs=[hbm()] * 7,
        out_specs=[hbm()] * 7,
        scratch_shapes=[pltpu.VMEM(r.shape, F32) for r in results] + [dma((2, 7))],
        compiler_params=pltpu.CompilerParams(vmem_limit_bytes=limit),
    )(*outs)
    layer_out, grad_hidden, grad_enc, grad_wq, grad_wk, grad_wv, grad_wo = outs
    return (
        layer_out,
        grad_hidden,
        grad_enc.reshape(encodings.shape),
        grad_wq,
        grad_wk,
        grad_wv,
        grad_wo,
    )


def solution(mesh):
    in_specs = (
        P("dp", "enc"),
        P("dp", None, "enc"),
        P("enc", None),
        P("enc", None),
        P("enc", None),
        P(None, "enc"),
        P("dp", "enc"),
        P("dp", None),
        P(),
    )
    out_specs = (
        P("dp", "enc"),
        P("dp", "enc"),
        P("dp", None, "enc"),
        P("enc", "dp"),
        P("enc", "dp"),
        P("enc", "dp"),
        P("dp", "enc"),
    )
    return jax.shard_map(
        per_device, mesh=mesh, in_specs=in_specs, out_specs=out_specs, check_vma=False
    )
```

time: 195 us -> 160 us (0.82)
  Pallas kernels: 181 us -> 158 us
  local copies, waits for them, and re-layouts: 12.4 us -> 1.34 us
    pallas_call x3 -> x2, Pallas kernels: 181 us -> 158 us  [the longest x1 153 us: per_device(): pl.pallas_call(layer_kernel, out_shape=results, in_specs=[pl.BlockSpec(me...]
    unnamed x14 -> x1, local copies, waits for them, and re-layouts: 12.4 us -> 1.34 us
where the time goes in v2:
time: 160 us
  Pallas kernels  158 us (99%)
    pallas_call x1, Pallas kernels, per_device(): pl.pallas_call(layer_kernel, out_shape=results, in_specs=[pl.BlockSpec(me...  153 us
    pallas_call x1, Pallas kernels, per_device(): pl.pallas_call(copy_kernel, out_shape=results, in_specs=[hbm()] * 7, out_...  5.07 us

profile of v2, /device:TPU:0, one launch (start us, length us, event | category | flops | bytes accessed | tf_op | source)
XLA Modules:
  0.0 160.2 jit_solution(15388635231114161904)
XLA Ops:
  0.6 1.3 copy.16.nbrs
  2.0 153.0 %shard_map.144 = (f32[256,512]{1,0:T(8,128)}, f32[256,512]{1,0:T(8,128)}, f32[256,512]{1,0:T(8,128)}, f32[512,512]{1,0:T(8,128)}, f32[512,512]{1,0:T(8,128)}, /*index=5*/f32[512,512]{1,0:T(8,128)}, f32[512,512]{1,0:T(8,128)}) custom-call(s32[4,2]{1,0:T(4,128)} %copy.16.nbrs, s32[16]{0:T(128)} %blocks.1, bf16[256,512]{1,0:T(8,128)(2,1)} %hidden.1, ...), custom_call_target="tpu_custom_call" | custom-call | tf_op jit(solution)/shard_map/pallas_call | solution.py:824
  155.0 5.1 %shard_map.145 = (f32[256,512]{1,0:T(8,128)}, f32[256,512]{1,0:T(8,128)}, f32[256,512]{1,0:T(8,128)}, f32[512,512]{1,0:T(8,128)}, f32[512,512]{1,0:T(8,128)}, /*index=5*/f32[512,512]{1,0:T(8,128)}, f32[512,512]{1,0:T(8,128)}) custom-call(f32[256,512]{1,0:T(8,128)} %get-tuple-element.21.refs_0_, f32[256,512]{1,0:T(8,128)} %get-tuple-element.22.refs_1_, ...), custom_call_target="tpu_custom_call" | custom-call | tf_op jit(solution)/shard_map/pallas_call | solution.py:876

commit v3 on v2

--- a/solution.py
+++ b/solution.py
@@ -649,123 +649,123 @@
     cots[y, c] = cotangent[...]
     encs[y, c] = encodings[...]
     hids[0] = hidden[...]
+    ring_q, ring_k = ring_of(1), ring_of(2)
     make_terms(0)
     place.meet(met)
     keys.step1()
-    gather_cots.first()
-    swap_hids = copies.start(hids.at[0], hids.at[1], place.partner)
     make_terms(1)
+    keys.step2()
+    gather_encs.first()
     values.step1()
-    gather_encs.first()
     make_terms(2)
-    keys.step2()
+    keys.step3()
+    values.step2()
+    keys.step4()
     query.step1()
-    values.step2()
-    gather_cots.second()
+    keys.finish(store_pair(0))
+    gather_keys.first()
     make_grad_terms()
-    keys.step3()
     values.step3()
-    grad.step1()
-    keys.step4()
-    gather_encs.second()
     query.step2()
     values.step4()
-    keys.finish(store_pair(0))
-    gather_keys.first()
+    grad.step1()
     values.finish(store_pair(1))
     gather_values.first()
-    swap_cots = swap(gather_cots, cots.at[:, c])
-    swap_encs = swap(gather_encs, encs.at[:, c])
-    query.step3()
     grad.step2()
     gather_keys.second()
+    query.step3()
+    gather_values.second()
+    swap_keys = swap(gather_keys, pair.at[0, :, c])
+    grad.step3()
+    swap_values = swap(gather_values, pair.at[1, :, c])
     query.step4()
-    gather_values.second()
-    grad.step3()
-    swap_keys = swap(gather_keys, pair.at[0, :, c])
+    gather_cots.first()
+    grad.step4()
     query.finish(store_to(queries))
-    swap_values = swap(gather_values, pair.at[1, :, c])
     swap_keys.wait_recv()
     swap_values.wait_recv()
     attend()
     net_h.step1()
-    grad.step4()
-    flip(prob)
-    net_h.step2()
     grad.finish(store_to(grads))
     attend_back()
     net_q.step1()
-    net_h.step3()
     gather_keys.flush()
     gather_values.flush()
     copies.flush([swap_keys, swap_values])
+    net_h.step2()
+    flip(prob)
     neighbour_grads(1, grads)
     swap_dense_v = swap_dense(1)
+    swap_hids = copies.start(hids.at[0], hids.at[1], place.partner)
+    net_q.step2()
+    gather_encs.second()
+    net_h.step3()
+    moves_dv = send_dense(1, swap_dense_v)
+    net_q.step3()
     flip(scored)
     neighbour_grads(0, queries)
     swap_dense_k = swap_dense(0)
-    net_q.step2()
-    moves_dv = send_dense(1, swap_dense_v)
+    sum_dense(1, moves_dv)
     moves_dk = send_dense(0, swap_dense_k)
-    net_q.step3()
+    net_v.step1()
+    net_h.step4()
+    net_v.step2()
+    sum_dense(0, moves_dk)
+    net_k.step1()
     swap_hids.wait_recv()
     for k in (0, 1):
         side_t[0, :, k * 256 : k * 256 + 256] = hids[k].T
-    net_h.step4()
-    sum_dense(1, moves_dv)
-    net_v.step1()
-    sum_dense(0, moves_dk)
-    net_k.step1()
     net_q.step4()
-    net_v.step2()
+    net_h.done()
     net_k.step2()
-    net_h.done()
+    for total in (keys, values, query, grad):
+        for ring in total.two:
+            ring.flush()
+    net_v.step3()
     moves_h = exchange(0, spread_h)
-    net_v.step3()
     net_q.done()
     swap_q = swap_half(1)
+    swap_encs = swap(gather_encs, encs.at[:, c])
     net_k.step3()
-    ring_q, ring_k = ring_of(1), ring_of(2)
     swap_q.wait_recv()
     weight_grad(1, ring_q)
+    net_v.step4()
+    net_k.step4()
+    net_v.done()
     for move in moves_h:
         move.wait_recv()
     net_sh.step1()
-    swap_encs.wait_recv()
-    side_t[1, :, 0:256] = encs[y, c].T
-    side_t[1, :, 256:512] = encs[y, 1 - c].T
-    net_v.step4()
-    net_k.step4()
-    net_sh.step2()
+    moves_v = exchange(3, spread_v)
+    gather_cots.second()
     accumulate(0, lambda b: mm(wide(0, b), out_weight[columns(b), :]))
-    net_v.done()
-    moves_v = exchange(3, spread_v)
     net_k.done()
-    swap_k = swap_half(2)
     ring_q.second()
     for move in moves_v:
         move.wait_recv()
     net_sv.step1()
+    swap_encs.wait_recv()
+    side_t[1, :, 0:256] = encs[y, c].T
+    side_t[1, :, 256:512] = encs[y, 1 - c].T
+    net_sh.step2()
+    swap_k = swap_half(2)
+    net_sv.step2()
     net_sh.step3()
     swap_k.wait_recv()
     weight_grad(2, ring_k)
-    net_sv.step2()
+    net_sv.step3()
+    turn(encs, store_encs)
+    net_sh.step4()
+    swap_cots = swap(gather_cots, cots.at[:, c])
+    accumulate(2, lambda b: transposed(2, 0, b) + transposed(3, 1, b))
     swap_cots.wait_recv()
-    for total in (keys, values, query, grad):
-        for ring in total.two:
-            ring.flush()
     turn(cots, store_cots)
-    net_sv.step3()
+    ring_k.second()
+    net_sv.step4()
     accumulate(1, lambda b: transposed(1, 2, b))
-    net_sh.step4()
-    turn(encs, store_encs)
     store_grad(1, ring_q)
-    accumulate(2, lambda b: transposed(2, 0, b) + transposed(3, 1, b))
-    net_sv.step4()
     net_sh.done()
     grads_out[1] = whole_grad(lambda b, j, i: sums[b, j, i], spread_h).T
     results[6].start()
-    ring_k.second()
     net_sv.done()
     results[6].wait()
     grads_out[1] = whole_grad(lambda b, j, i: r1a[b, j, i // 2, i % 2], spread_v)

time: 160 us -> 149 us (0.931)
  Pallas kernels: 158 us -> 147 us
    pallas_call x1, Pallas kernels: 153 us -> 142 us  [per_device(): pl.pallas_call(layer_kernel, out_shape=results, in_specs=[pl.BlockSpec(me...]
where the time goes in v3:
time: 149 us
  Pallas kernels  147 us (99%)
    pallas_call x1, Pallas kernels, per_device(): pl.pallas_call(layer_kernel, out_shape=results, in_specs=[pl.BlockSpec(me...  142 us
    pallas_call x1, Pallas kernels, per_device(): pl.pallas_call(copy_kernel, out_shape=results, in_specs=[hbm()] * 7, out_...  5.07 us

profile of v3, /device:TPU:0, one launch (start us, length us, event | category | flops | bytes accessed | tf_op | source)
XLA Modules:
  0.0 149.1 jit_solution(13927937738318444283)
XLA Ops:
  0.6 1.3 copy.16.nbrs
  2.0 141.9 %shard_map.144 = (f32[256,512]{1,0:T(8,128)}, f32[256,512]{1,0:T(8,128)}, f32[256,512]{1,0:T(8,128)}, f32[512,512]{1,0:T(8,128)}, f32[512,512]{1,0:T(8,128)}, /*index=5*/f32[512,512]{1,0:T(8,128)}, f32[512,512]{1,0:T(8,128)}) custom-call(s32[4,2]{1,0:T(4,128)} %copy.16.nbrs, s32[16]{0:T(128)} %blocks.1, bf16[256,512]{1,0:T(8,128)(2,1)} %hidden.1, ...), custom_call_target="tpu_custom_call" | custom-call | tf_op jit(solution)/shard_map/pallas_call | solution.py:824
  143.9 5.1 %shard_map.145 = (f32[256,512]{1,0:T(8,128)}, f32[256,512]{1,0:T(8,128)}, f32[256,512]{1,0:T(8,128)}, f32[512,512]{1,0:T(8,128)}, f32[512,512]{1,0:T(8,128)}, /*index=5*/f32[512,512]{1,0:T(8,128)}, f32[512,512]{1,0:T(8,128)}) custom-call(f32[256,512]{1,0:T(8,128)} %get-tuple-element.21.refs_0_, f32[256,512]{1,0:T(8,128)} %get-tuple-element.22.refs_1_, ...), custom_call_target="tpu_custom_call" | custom-call | tf_op jit(solution)/shard_map/pallas_call | solution.py:876

commit v4 on v2

--- a/solution.py
+++ b/solution.py
@@ -188,9 +188,14 @@
             RingSum(copies, place, "x", lower_two, r1b.at[1], r2b.at[1]),
         )
 
-    def step1(self):
+    def opposite(self):
         for ring in self.one:
-            ring.first()
+            ring.send_opposite()
+
+    def sides(self):
+        for ring in self.one:
+            ring.send_right()
+            ring.send_left()
 
     def step2(self):
         for ring in self.one:
@@ -307,15 +312,18 @@
     prob,
     scored,
     flipped,
-    spread_h,
     spread_v,
+    spread_q,
     theirs,
+    theirs_q,
     side_t,
     dense_in,
     dense_sum,
     dense_r,
     part_r1,
     part_r2,
+    half_r1,
+    half_r2,
     rows_out,
     grads_out,
     load_sems,
@@ -331,27 +339,35 @@
         pltpu.make_async_copy(src, dst, load_sems.at[k])
         for k, (src, dst) in enumerate(
             [
-                (wk_hbm, weights.at[0]),
                 (wv_hbm, weights.at[1]),
                 (wq_hbm, weights.at[2]),
                 (wo_hbm, out_weight),
             ]
         )
     ]
-    for load in loads:
-        load.start()
+    pieces = [
+        pltpu.make_async_copy(
+            wk_hbm.at[:, 1024 * b : 1024 * b + 1024],
+            weights.at[0, :, 1024 * b : 1024 * b + 1024],
+            load_sems.at[10 + b],
+        )
+        for b in range(4)
+    ]
+    for piece in pieces:
+        piece.start()
+    loads[0].start()
     place.greet(met)
     results = [
-        pltpu.make_async_copy(src, dst, load_sems.at[4 + k])
+        pltpu.make_async_copy(src, dst, load_sems.at[3 + k])
         for k, (src, dst) in enumerate(
             [
                 (rows_out.at[0], layer_hbm),
                 (rows_out.at[1], grad_hidden_hbm),
                 (rows_out.at[2], grad_encodings_hbm),
                 (grads_out.at[0], grad_wq_hbm),
-                (grads_out.at[0], grad_wk_hbm),
-                (grads_out.at[1], grad_wv_hbm),
-                (grads_out.at[1], grad_wo_hbm),
+                (grads_out.at[1], grad_wk_hbm),
+                (grads_out.at[2], grad_wv_hbm),
+                (grads_out.at[3], grad_wo_hbm),
             ]
         )
     ]
@@ -364,8 +380,17 @@
         for k in range(4)
     ]
 
+    def first_terms():
+        for b in range(4):
+            pieces[b].wait()
+            product = mm(encodings[...], weights[0, :, 1024 * b : 1024 * b + 1024]).astype(BF16)
+            for i in range(4):
+                terms[0, b, i] = product[:, i * 256 : i * 256 + 256]
+        loads[1].start()
+        loads[2].start()
+
     def make_terms(k):
-        loads[k].wait()
+        loads[k - 1].wait()
         rows = left[k][...]
 
         def body(b, carry):
@@ -377,7 +402,7 @@
         lax.fori_loop(0, 4, body, 0)
 
     def make_grad_terms():
-        loads[3].wait()
+        loads[2].wait()
         rows = cotangent[...]
 
         def body(b, carry):
@@ -408,8 +433,8 @@
 
         return block
 
-    gather_cots = RingGather(copies, place, "y", row_block(cots))
     gather_encs = RingGather(copies, place, "y", row_block(encs))
+    gather_hids = RingGather(copies, place, "y", row_block(hids))
     gather_keys, gather_values = [
         RingGather(copies, place, "y", pair_block(k)) for k in (0, 1)
     ]
@@ -441,7 +466,7 @@
         return jnp.concatenate(
             [
                 pair[which, n // 4, (n // 2) % 2, n % 2, :, h * 128 : h * 128 + 128]
-                for n in (nbrs[t, 0], nbrs[t, 1])
+                for n in (nbrs[0, t], nbrs[1, t])
             ],
             axis=0,
         )
@@ -449,8 +474,8 @@
     def attend():
         slot = lax.broadcasted_iota(jnp.int32, (64, 256), 1)
         for i, (t, h) in enumerate(cases):
-            limit0 = BLK * blocks[nbrs[t, 0]]
-            limit1 = BLK * blocks[nbrs[t, 1]]
+            limit0 = BLK * blocks[nbrs[0, t]]
+            limit1 = BLK * blocks[nbrs[1, t]]
             valid = slot < jnp.where(slot < 128, limit0, limit1 + 128)
             scores = (
                 lax.dot_general(
@@ -486,9 +511,9 @@
         lane = lax.broadcasted_iota(jnp.int32, (128, 256), 1)
         names = []
         for j in range(2):
-            name = jnp.where(lane < 64, nbrs[0, j], nbrs[1, j])
-            name = jnp.where(lane < 128, name, nbrs[2, j])
-            names.append(jnp.where(lane < 192, name, nbrs[3, j]))
+            name = jnp.where(lane < 64, nbrs[j, 0], nbrs[j, 1])
+            name = jnp.where(lane < 128, name, nbrs[j, 2])
+            names.append(jnp.where(lane < 192, name, nbrs[j, 3]))
 
         def body(i, carry):
             for h in range(2):
@@ -506,20 +531,24 @@
                 ).astype(BF16)
                 term = mm(chosen, rows[:, h * 128 : h * 128 + 128]).astype(BF16)
                 for j in range(2):
-                    pair[which, i // 2, i % 2, j, :, h * 128 : h * 128 + 128] = term[
-                        j * 128 : j * 128 + 128
-                    ]
+                    sums[
+                        2 * which + i // 4, (i // 2) % 2, 2 * (i % 2) + j, :, h * 128 : h * 128 + 128
+                    ] = term[j * 128 : j * 128 + 128]
             return carry
 
         lax.fori_loop(0, 8, body, 0)
 
     def swap_dense(k):
-        return copies.start(pair.at[k, :, 1 - c], dense_in.at[k], place.partner)
+        return copies.start(
+            sums.at[2 * k : 2 * k + 2, :, pl.ds(2 * (1 - c), 2)], dense_in.at[k], place.partner
+        )
 
     def send_dense(k, swapped):
         swapped.wait_recv()
         for b in range(4):
-            dense_sum[b, k] = (pair[k, b, c].astype(F32) + dense_in[k, b].astype(F32)).astype(BF16)
+            mine = sums[2 * k + b // 2, b % 2, pl.ds(2 * c, 2)]
+            theirs_too = dense_in[k, b // 2, b % 2]
+            dense_sum[b, k] = (mine.astype(F32) + theirs_too.astype(F32)).astype(BF16)
         return [
             copies.start(
                 dense_sum.at[(y + step) % 4, k],
@@ -538,56 +567,84 @@
         terms[2 + k, x, z] = total.astype(BF16).reshape(256, 256)
 
     net_h, net_q, net_k, net_v = [PlaneGather(copies, place, terms.at[k]) for k in range(4)]
-    net_sh, net_sv = [PlaneGather(copies, place, ref) for ref in (spread_h, spread_v)]
+    net_sv, net_sq = [PlaneGather(copies, place, ref) for ref in (spread_v, spread_q)]
 
     def swap_half(k):
-        return copies.start(terms.at[k, :, pl.ds(2 * (1 - c), 2)], theirs.at[k - 1], place.partner)
-
-    def ring_of(k):
-        def part(b, h):
-            return r2a.at[2 * (k - 1) + b // 2, b % 2, h]
-
-        return RingSum(copies, place, "y", part, part_r1.at[k - 1], part_r2.at[k - 1])
-
-    def weight_grad(k, ring):
-        def block(b):
-            own = jnp.concatenate([terms[k, b, 2 * c + i] for i in (0, 1)], axis=1)
-            other = jnp.concatenate([theirs[k - 1, b, i] for i in (0, 1)], axis=1)
+        return copies.start(terms.at[2 * k, :, pl.ds(2 * (1 - c), 2)], theirs.at[k], place.partner)
+
+    class WeightGrad:
+        def __init__(self, k):
+            def part(b, h):
+                return r2a.at[2 * k + b // 2, b % 2, h]
+
+            self.k = k
+            self.ring = RingSum(copies, place, "y", part, part_r1.at[k], part_r2.at[k])
+
+        def block(self, b):
+            k = self.k
+            own = jnp.concatenate([terms[2 * k, b, 2 * c + i] for i in (0, 1)], axis=1)
+            other = jnp.concatenate([theirs[k, b, i] for i in (0, 1)], axis=1)
             both = jnp.concatenate([own, other], axis=0)
-            product = mm(side_t[k - 1], both).astype(BF16)
+            product = mm(side_t[2 * k], both).astype(BF16)
             for h in (0, 1):
                 for i in (0, 1):
                     quarter = product[256 * h : 256 * h + 256, 256 * i : 256 * i + 256]
-                    r2a[2 * (k - 1) + b // 2, b % 2, h, i] = quarter.reshape(2, 128, 256)
-
-        block(ring.opp)
-        ring.send_opposite()
-        block(ring.rt)
-        ring.send_right()
-        block(ring.lf)
-        ring.send_left()
-        block(ring.pos)
-
-    def store_grad(k, ring):
-        for h, found in enumerate(ring.total()):
-            for i in (0, 1):
-                grads_out[0, 256 * h : 256 * h + 256, 256 * i : 256 * i + 256] = found[i].reshape(
-                    256, 256
-                )
-        results[2 + k].start()
+                    r2a[2 * k + b // 2, b % 2, h, i] = quarter.reshape(2, 128, 256)
+
+        def one(self):
+            self.block(self.ring.opp)
+            self.ring.send_opposite()
+
+        def two(self):
+            self.block(self.ring.rt)
+            self.ring.send_right()
+
+        def three(self):
+            self.block(self.ring.lf)
+            self.ring.send_left()
+
+        def four(self):
+            self.block(self.ring.pos)
+
+        def store(self):
+            for h, found in enumerate(self.ring.total()):
+                for i in (0, 1):
+                    square = found[i].reshape(256, 256)
+                    if self.k == 0:
+                        grads_out[3, 256 * i : 256 * i + 256, 256 * h : 256 * h + 256] = square.T
+                    else:
+                        grads_out[1, 256 * h : 256 * h + 256, 256 * i : 256 * i + 256] = square
+            results[6 if self.k == 0 else 4].start()
+
+    class QueryGrad(WeightGrad):
+        def __init__(self):
+            def part(b, h):
+                return pair.at[0, b, h]
+
+            self.ring = RingSum(copies, place, "y", part, half_r1, half_r2)
+
+        def block(self, b):
+            both = jnp.concatenate([terms[1, b, 2 * c], theirs_q[b]], axis=0)
+            product = mm(side_t[1], both).astype(BF16)
+            pair[0, b] = product.reshape(2, 2, 128, 256)
+
+        def store(self):
+            for h, found in enumerate(self.ring.total()):
+                grads_out[0, 256 * h : 256 * h + 256, 0:256] = found.reshape(256, 256)
 
     def wide(k, b):
         return jnp.concatenate([terms[k, b, i] for i in range(4)], axis=1)
 
-    def accumulate(k, make):
-        rows_out[k] = make(0)
-
+    def accumulate(k, make, add=False, last=True):
         def body(b, carry):
             rows_out[k] += make(b)
             return carry
 
-        lax.fori_loop(1, 4, body, 0)
-        results[k].start()
+        if not add:
+            rows_out[k] = make(0)
+        lax.fori_loop(0 if add else 1, 4, body, 0)
+        if last:
+            results[k].start()
 
     def transposed(k, slot, b):
         return lax.dot_general(
@@ -605,174 +662,212 @@
 
         lax.fori_loop(0, 8, body, 0)
 
-    def store_cots(t, found):
-        for i in range(4):
-            sums[t // 2, t % 2, i] = found[128 * i : 128 * i + 128]
-
     def store_encs(t, found):
         for i in range(4):
             r1a[t // 2, t % 2, i // 2, i % 2] = found[128 * i : 128 * i + 128]
 
-    def exchange(k, spread):
+    def store_hids(t, found):
+        for i in range(4):
+            sums[t // 2, t % 2, i] = found[128 * i : 128 * i + 128]
+
+    def exchange_values():
         span = pl.ds(pl.multiple_of(place.enc * 16, 16), 16)
-        moves = [
+        spread_v[x, z, place.dp] = terms[3, y, pl.ds(2 * c, 2), span]
+        return [
             copies.start(
-                terms.at[k, oy, pl.ds(2 * oc, 2), span],
-                spread.at[x, z, place.dp],
+                terms.at[3, oy, pl.ds(2 * oc, 2), span],
+                spread_v.at[x, z, place.dp],
                 (oy * 2 + oc, place.enc),
             )
             for oy, oc in column
         ]
-        spread[x, z, place.dp] = terms[k, y, pl.ds(2 * c, 2), span]
-        return moves
-
-    def whole_grad(turned, spread):
+
+    def exchange_queries():
+        span = pl.ds(pl.multiple_of(place.enc * 16, 16), 16)
+        spread_q[x, z, place.dp] = terms[1, y, 2 * c + 1, span]
+        return [
+            copies.start(
+                terms.at[1, oy, 2 * oc + 1, span],
+                spread_q.at[x, z, place.dp],
+                (oy * 2 + oc, place.enc),
+            )
+            for oy, oc in column
+        ]
+
+    def whole_grad(turned, rows_of_part):
         total = None
         for b in range(4):
             sides = jnp.concatenate(
                 [
-                    jnp.concatenate([turned(b, j, i) for j in (0, 1)], axis=1) for i in range(4)
+                    jnp.concatenate([turned(b, j, i) for j in (0, 1)], axis=1)
+                    for i in range(4)
                 ],
                 axis=0,
             )
-            rows = jnp.concatenate(
-                [
-                    jnp.concatenate([spread[b, k, :, i].reshape(128, 256) for i in (0, 1)], axis=1)
-                    for k in range(4)
-                ],
-                axis=0,
-            )
+            rows = jnp.concatenate([rows_of_part(b, k) for k in range(4)], axis=0)
             term = mm(sides, rows)
             total = term if total is None else total + term
         return total
 
-    cots[y, c] = cotangent[...]
+    def value_rows(b, k):
+        return jnp.concatenate([spread_v[b, k, :, i].reshape(128, 256) for i in (0, 1)], axis=1)
+
+    def query_rows(b, k):
+        return spread_q[b, k].reshape(128, 256)
+
+    def turned_encs(b, j, i):
+        return r1a[b, j, i // 2, i % 2]
+
+    def turned_hids(b, j, i):
+        return sums[b, j, i]
+
+    cots[0] = cotangent[...]
     encs[y, c] = encodings[...]
-    hids[0] = hidden[...]
-    make_terms(0)
+    hids[y, c] = hidden[...]
+    work_h, work_k, work_q = WeightGrad(0), WeightGrad(1), QueryGrad()
+    first_terms()
     place.meet(met)
-    keys.step1()
-    gather_cots.first()
-    swap_hids = copies.start(hids.at[0], hids.at[1], place.partner)
+    keys.opposite()
     make_terms(1)
-    values.step1()
+    values.opposite()
+    keys.step2()
+    keys.sides()
     gather_encs.first()
     make_terms(2)
-    keys.step2()
-    query.step1()
+    gather_hids.first()
+    values.sides()
     values.step2()
-    gather_cots.second()
-    make_grad_terms()
     keys.step3()
+    query.opposite()
+    keys.step4()
     values.step3()
-    grad.step1()
-    keys.step4()
-    gather_encs.second()
+    query.sides()
+    values.step4()
     query.step2()
-    values.step4()
     keys.finish(store_pair(0))
     gather_keys.first()
+    make_grad_terms()
     values.finish(store_pair(1))
     gather_values.first()
-    swap_cots = swap(gather_cots, cots.at[:, c])
-    swap_encs = swap(gather_encs, encs.at[:, c])
+    grad.opposite()
+    gather_keys.second()
     query.step3()
+    gather_values.second()
+    grad.sides()
+    query.step4()
     grad.step2()
-    gather_keys.second()
-    query.step4()
-    gather_values.second()
-    grad.step3()
     swap_keys = swap(gather_keys, pair.at[0, :, c])
+    swap_values = swap(gather_values, pair.at[1, :, c])
     query.finish(store_to(queries))
-    swap_values = swap(gather_values, pair.at[1, :, c])
     swap_keys.wait_recv()
     swap_values.wait_recv()
     attend()
     net_h.step1()
+    gather_encs.second()
+    grad.step3()
+    net_h.step2()
+    gather_hids.second()
     grad.step4()
     flip(prob)
-    net_h.step2()
+    net_h.step3()
+    swap_cots = copies.start(cots.at[0], cots.at[1], place.partner)
     grad.finish(store_to(grads))
-    attend_back()
-    net_q.step1()
-    net_h.step3()
-    gather_keys.flush()
-    gather_values.flush()
-    copies.flush([swap_keys, swap_values])
+    for total in (keys, values, query, grad):
+        for ring in total.two:
+            ring.flush()
     neighbour_grads(1, grads)
     swap_dense_v = swap_dense(1)
+    attend_back()
+    moves_dv = send_dense(1, swap_dense_v)
+    net_q.step1()
+    net_h.step4()
+    swap_encs = swap(gather_encs, encs.at[:, c])
     flip(scored)
     neighbour_grads(0, queries)
     swap_dense_k = swap_dense(0)
     net_q.step2()
-    moves_dv = send_dense(1, swap_dense_v)
-    moves_dk = send_dense(0, swap_dense_k)
-    net_q.step3()
-    swap_hids.wait_recv()
-    for k in (0, 1):
-        side_t[0, :, k * 256 : k * 256 + 256] = hids[k].T
-    net_h.step4()
     sum_dense(1, moves_dv)
     net_v.step1()
+    moves_dk = send_dense(0, swap_dense_k)
+    net_h.done()
+    net_q.step3()
+    swap_h = swap_half(0)
+    swap_cots.wait_recv()
+    for k in (0, 1):
+        side_t[0, :, k * 256 : k * 256 + 256] = cots[k].T
+    net_v.step2()
+    swap_h.wait_recv()
+    work_h.one()
+    swap_hids = swap(gather_hids, hids.at[:, c])
+    work_h.two()
+    work_h.three()
     sum_dense(0, moves_dk)
     net_k.step1()
     net_q.step4()
-    net_v.step2()
+    gather_keys.flush()
+    gather_values.flush()
+    copies.flush([swap_keys, swap_values])
     net_k.step2()
-    net_h.done()
-    moves_h = exchange(0, spread_h)
     net_v.step3()
     net_q.done()
-    swap_q = swap_half(1)
+    work_h.ring.second()
+    swap_hids.wait_recv()
+    side_t[1, :, 0:256] = hids[y, c].T
+    side_t[1, :, 256:512] = hids[y, 1 - c].T
+    swap_q = copies.start(terms.at[1, :, 2 * (1 - c)], theirs_q, place.partner)
     net_k.step3()
-    ring_q, ring_k = ring_of(1), ring_of(2)
+    swap_encs.wait_recv()
+    side_t[2, :, 0:256] = encs[y, c].T
+    side_t[2, :, 256:512] = encs[y, 1 - c].T
+    work_h.four()
+    accumulate(1, lambda b: transposed(1, 2, b))
+    net_v.step4()
     swap_q.wait_recv()
-    weight_grad(1, ring_q)
-    for move in moves_h:
+    work_q.one()
+    copies.flush([swap_dense_v, swap_dense_k])
+    turn(hids, store_hids)
+    work_h.store()
+    work_q.two()
+    moves_q = exchange_queries()
+    net_k.step4()
+    work_q.three()
+    net_v.done()
+    moves_v = exchange_values()
+    for move in moves_q:
         move.wait_recv()
-    net_sh.step1()
-    swap_encs.wait_recv()
-    side_t[1, :, 0:256] = encs[y, c].T
-    side_t[1, :, 256:512] = encs[y, 1 - c].T
-    net_v.step4()
-    net_k.step4()
-    net_sh.step2()
-    accumulate(0, lambda b: mm(wide(0, b), out_weight[columns(b), :]))
-    net_v.done()
-    moves_v = exchange(3, spread_v)
+    net_sq.step1()
     net_k.done()
-    swap_k = swap_half(2)
-    ring_q.second()
+    swap_k = swap_half(1)
     for move in moves_v:
         move.wait_recv()
     net_sv.step1()
-    net_sh.step3()
+    work_q.ring.second()
+    accumulate(2, lambda b: transposed(3, 1, b), last=False)
+    net_sq.step2()
     swap_k.wait_recv()
-    weight_grad(2, ring_k)
+    work_k.one()
     net_sv.step2()
-    swap_cots.wait_recv()
-    for total in (keys, values, query, grad):
-        for ring in total.two:
-            ring.flush()
-    turn(cots, store_cots)
+    net_sq.step3()
+    work_k.two()
+    work_k.three()
+    work_q.four()
     net_sv.step3()
-    accumulate(1, lambda b: transposed(1, 2, b))
-    net_sh.step4()
+    net_sq.step4()
+    work_k.ring.second()
+    work_k.four()
     turn(encs, store_encs)
-    store_grad(1, ring_q)
-    accumulate(2, lambda b: transposed(2, 0, b) + transposed(3, 1, b))
+    accumulate(0, lambda b: mm(wide(0, b), out_weight[columns(b), :]))
     net_sv.step4()
-    net_sh.done()
-    grads_out[1] = whole_grad(lambda b, j, i: sums[b, j, i], spread_h).T
-    results[6].start()
-    ring_k.second()
+    work_q.store()
+    accumulate(2, lambda b: transposed(2, 0, b), add=True)
+    net_sq.done()
+    grads_out[0, :, 256:512] = whole_grad(turned_hids, query_rows)
     net_sv.done()
-    results[6].wait()
-    grads_out[1] = whole_grad(lambda b, j, i: r1a[b, j, i // 2, i % 2], spread_v)
+    results[3].start()
+    grads_out[2] = whole_grad(turned_encs, value_rows)
     results[5].start()
-    results[3].wait()
-    store_grad(2, ring_k)
-    for k in (0, 1, 2, 4, 5):
+    work_k.store()
+    for k in range(7):
         results[k].wait()
     copies.finish()
 
@@ -836,26 +931,29 @@
             pltpu.VMEM((4, 2, 2, 64, 256), BF16),
             pltpu.VMEM((4, 2, 2, 2, 64, 256), BF16),
             pltpu.VMEM((2, 4, 2, 2, 128, 256), BF16),
+            pltpu.VMEM((2, 256, 512), BF16),
             pltpu.VMEM((4, 2, 256, 512), BF16),
             pltpu.VMEM((4, 2, 256, 512), BF16),
-            pltpu.VMEM((2, 256, 512), BF16),
             pltpu.VMEM((256, 256), BF16),
             pltpu.VMEM((256, 256), BF16),
             pltpu.VMEM((2, 256, 256), F32),
             pltpu.VMEM((2, 256, 256), F32),
             pltpu.VMEM((2, 256, 256), F32),
             pltpu.VMEM((4, 4, 8, 2, 16, 256), BF16),
-            pltpu.VMEM((4, 4, 8, 2, 16, 256), BF16),
+            pltpu.VMEM((4, 4, 8, 16, 256), BF16),
             pltpu.VMEM((2, 4, 2, 256, 256), BF16),
-            pltpu.VMEM((2, 512, 512), BF16),
-            pltpu.VMEM((2, 4, 2, 128, 256), BF16),
+            pltpu.VMEM((4, 256, 256), BF16),
+            pltpu.VMEM((3, 512, 512), BF16),
+            pltpu.VMEM((2, 2, 2, 2, 128, 256), BF16),
             pltpu.VMEM((4, 2, 2, 128, 256), BF16),
             pltpu.VMEM((3, 2, 2, 128, 256), BF16),
             pltpu.VMEM((2, 2, 2, 2, 128, 256), BF16),
             pltpu.VMEM((2, 2, 2, 2, 2, 128, 256), BF16),
+            pltpu.VMEM((2, 2, 128, 256), BF16),
+            pltpu.VMEM((2, 2, 2, 128, 256), BF16),
             pltpu.VMEM((3, 256, 512), F32),
-            pltpu.VMEM((2, 512, 512), F32),
-            dma((11,)),
+            pltpu.VMEM((4, 512, 512), F32),
+            dma((14,)),
             dma((256,)),
             dma((256,)),
         ],
@@ -863,7 +961,7 @@
             collective_id=0, has_side_effects=True, vmem_limit_bytes=limit
         ),
     )(
-        stretch_nbrs,
+        stretch_nbrs.T,
         nbr_blocks,
         hidden,
         flat_enc,

time: 160 us -> 143 us (0.89)
  Pallas kernels: 158 us -> 142 us
    pallas_call x1, Pallas kernels: 153 us -> 137 us  [per_device(): pl.pallas_call(layer_kernel, out_shape=results, in_specs=[pl.BlockSpec(me...]
where the time goes in v4:
time: 143 us; the launch traced here: 142 us
  Pallas kernels  142 us (99%)
    pallas_call x1, Pallas kernels, per_device(): pl.pallas_call(layer_kernel, out_shape=results, in_specs=[pl.BlockSpec(me...  137 us
    pallas_call x1, Pallas kernels, per_device(): pl.pallas_call(copy_kernel, out_shape=results, in_specs=[hbm()] * 7, out_...  5.07 us

profile of v4, /device:TPU:0, one launch (start us, length us, event | category | flops | bytes accessed | tf_op | source)
XLA Modules:
  0.0 142.4 jit_solution(1440254066346695631)
XLA Ops:
  0.6 136.6 %shard_map.144 = (f32[256,512]{1,0:T(8,128)}, f32[256,512]{1,0:T(8,128)}, f32[256,512]{1,0:T(8,128)}, f32[512,512]{1,0:T(8,128)}, f32[512,512]{1,0:T(8,128)}, /*index=5*/f32[512,512]{1,0:T(8,128)}, f32[512,512]{1,0:T(8,128)}) custom-call(s32[2,4]{1,0:T(2,128)} %bitcast.4, s32[16]{0:T(128)} %blocks.1, bf16[256,512]{1,0:T(8,128)(2,1)} %hidden.1, ...), custom_call_target="tpu_custom_call" | custom-call | tf_op jit(solution)/shard_map/pallas_call | solution.py:919
  137.2 5.1 %shard_map.145 = (f32[256,512]{1,0:T(8,128)}, f32[256,512]{1,0:T(8,128)}, f32[256,512]{1,0:T(8,128)}, f32[512,512]{1,0:T(8,128)}, f32[512,512]{1,0:T(8,128)}, /*index=5*/f32[512,512]{1,0:T(8,128)}, f32[512,512]{1,0:T(8,128)}) custom-call(f32[256,512]{1,0:T(8,128)} %get-tuple-element.21.refs_0_, f32[256,512]{1,0:T(8,128)} %get-tuple-element.22.refs_1_, ...), custom_call_target="tpu_custom_call" | custom-call | tf_op jit(solution)/shard_map/pallas_call | solution.py:974

commit v5 on v4

--- a/solution.py
+++ b/solution.py
@@ -223,59 +223,78 @@
 
 class PlaneGather:
     def __init__(self, copies, place, buf):
-        x, z = place.pos["x"], place.pos["z"]
+        self.copies = copies
         half = buf.shape[2] // 2
+        self.ways = [self.way(copies, place, buf, half, k) for k in (0, 1)]
+
+    def way(self, copies, place, buf, half, k):
+        axes = ("x", "z") if k == 0 else ("z", "x")
+        near, far = [place.pos[axis] for axis in axes]
         quarter = half // 2
-
-        def upper(b, h):
+        start = k * half
+
+        def cells(i, j, rows):
+            return buf.at[i, j, rows] if k == 0 else buf.at[j, i, rows]
+
+        def block(b, h):
             if h is None:
-                return buf.at[b, z, 0:half]
-            return buf.at[b, z, quarter * h : quarter * h + quarter]
-
-        def lower(b, h):
-            if h is None:
-                return buf.at[x, b, half : 2 * half]
-            return buf.at[x, b, half + quarter * h : half + quarter * h + quarter]
-
-        def upper_two(b, h):
-            if h is None:
-                return buf.at[:, b, 0:half]
-            return buf.at[2 * h : 2 * h + 2, b, 0:half]
-
-        def lower_two(b, h):
-            if h is None:
-                return buf.at[b, :, half : 2 * half]
-            return buf.at[b, 2 * h : 2 * h + 2, half : 2 * half]
-
-        self.one = (
-            RingGather(copies, place, "x", upper),
-            RingGather(copies, place, "z", lower),
-        )
-        self.two = (
-            RingGather(copies, place, "z", upper_two),
-            RingGather(copies, place, "x", lower_two),
-        )
+                return cells(b, far, slice(start, start + half))
+            low = start + quarter * h
+            return cells(b, far, slice(low, low + quarter))
+
+        def pair_of(h, j):
+            return cells(slice(2 * h, 2 * h + 2), j, slice(start, start + half))
+
+        return {
+            "ring": RingGather(copies, place, axes[0], block),
+            "block": block,
+            "pair": pair_of,
+            "near": near,
+            "far": far,
+            "right": place.right[axes[1]],
+            "left": place.left[axes[1]],
+            "from_left": [],
+            "from_right": [],
+        }
+
+    def send(self, way, step):
+        cell = way["block"]((way["near"] + step) % 4, None)
+        way["from_left"].append(self.copies.start(cell, cell, way["right"]))
+        way["from_right"].append(self.copies.start(cell, cell, way["left"]))
 
     def step1(self):
-        for ring in self.one:
-            ring.first()
+        for way in self.ways:
+            way["ring"].first()
+        for way in self.ways:
+            self.send(way, 0)
 
     def step2(self):
-        for ring in self.one:
-            ring.second()
+        for way in self.ways:
+            way["ring"].second()
+        for way in self.ways:
+            self.send(way, 1)
+            self.send(way, 3)
 
     def step3(self):
-        for one, two in zip(self.one, self.two):
-            one.done()
-            two.first()
+        for way in self.ways:
+            way["ring"].done()
+            self.send(way, 2)
 
     def step4(self):
-        for ring in self.two:
-            ring.second()
+        for way in self.ways:
+            for copy in way["from_left"]:
+                copy.wait_recv()
+            part = way["pair"](0, (way["far"] + 3) % 4)
+            way["d"] = self.copies.start(part, part, way["right"])
+            for copy in way["from_right"]:
+                copy.wait_recv()
+            part = way["pair"](1, (way["far"] + 1) % 4)
+            way["e"] = self.copies.start(part, part, way["left"])
 
     def done(self):
-        for ring in self.two:
-            ring.done()
+        for way in self.ways:
+            way["d"].wait_recv()
+            way["e"].wait_recv()
 
 
 def layer_kernel(
@@ -730,137 +749,137 @@
     keys.opposite()
     make_terms(1)
     values.opposite()
+    keys.sides()
+    gather_hids.first()
     keys.step2()
-    keys.sides()
+    values.sides()
+    make_terms(2)
+    gather_hids.second()
+    values.step2()
+    make_grad_terms()
     gather_encs.first()
-    make_terms(2)
-    gather_hids.first()
-    values.sides()
-    values.step2()
     keys.step3()
     query.opposite()
     keys.step4()
     values.step3()
     query.sides()
+    keys.finish(store_pair(0))
+    gather_encs.second()
     values.step4()
+    gather_keys.first()
     query.step2()
-    keys.finish(store_pair(0))
-    gather_keys.first()
-    make_grad_terms()
     values.finish(store_pair(1))
     gather_values.first()
     grad.opposite()
+    grad.sides()
     gather_keys.second()
     query.step3()
     gather_values.second()
-    grad.sides()
+    grad.step2()
     query.step4()
-    grad.step2()
+    swap_values = swap(gather_values, pair.at[1, :, c])
     swap_keys = swap(gather_keys, pair.at[0, :, c])
-    swap_values = swap(gather_values, pair.at[1, :, c])
+    grad.step3()
     query.finish(store_to(queries))
     swap_keys.wait_recv()
     swap_values.wait_recv()
     attend()
     net_h.step1()
-    gather_encs.second()
-    grad.step3()
+    swap_hids = swap(gather_hids, hids.at[:, c])
+    grad.step4()
     net_h.step2()
-    gather_hids.second()
-    grad.step4()
     flip(prob)
-    net_h.step3()
-    swap_cots = copies.start(cots.at[0], cots.at[1], place.partner)
     grad.finish(store_to(grads))
     for total in (keys, values, query, grad):
         for ring in total.two:
             ring.flush()
+    attend_back()
+    net_h.step3()
     neighbour_grads(1, grads)
     swap_dense_v = swap_dense(1)
-    attend_back()
-    moves_dv = send_dense(1, swap_dense_v)
     net_q.step1()
-    net_h.step4()
-    swap_encs = swap(gather_encs, encs.at[:, c])
     flip(scored)
     neighbour_grads(0, queries)
     swap_dense_k = swap_dense(0)
+    net_h.step4()
+    moves_dv = send_dense(1, swap_dense_v)
     net_q.step2()
-    sum_dense(1, moves_dv)
-    net_v.step1()
+    swap_cots = copies.start(cots.at[0], cots.at[1], place.partner)
     moves_dk = send_dense(0, swap_dense_k)
     net_h.done()
+    swap_h = swap_half(0)
     net_q.step3()
-    swap_h = swap_half(0)
     swap_cots.wait_recv()
     for k in (0, 1):
         side_t[0, :, k * 256 : k * 256 + 256] = cots[k].T
-    net_v.step2()
+    sum_dense(1, moves_dv)
+    swap_hids.wait_recv()
+    side_t[1, :, 0:256] = hids[y, c].T
+    side_t[1, :, 256:512] = hids[y, 1 - c].T
+    net_v.step1()
     swap_h.wait_recv()
     work_h.one()
-    swap_hids = swap(gather_hids, hids.at[:, c])
+    net_q.step4()
     work_h.two()
-    work_h.three()
-    sum_dense(0, moves_dk)
-    net_k.step1()
-    net_q.step4()
     gather_keys.flush()
     gather_values.flush()
     copies.flush([swap_keys, swap_values])
+    sum_dense(0, moves_dk)
+    net_k.step1()
+    work_h.three()
+    net_q.done()
+    net_v.step2()
+    swap_encs = swap(gather_encs, encs.at[:, c])
+    work_h.ring.second()
     net_k.step2()
-    net_v.step3()
-    net_q.done()
-    work_h.ring.second()
-    swap_hids.wait_recv()
-    side_t[1, :, 0:256] = hids[y, c].T
-    side_t[1, :, 256:512] = hids[y, 1 - c].T
+    moves_q = exchange_queries()
     swap_q = copies.start(terms.at[1, :, 2 * (1 - c)], theirs_q, place.partner)
     net_k.step3()
+    net_v.step3()
+    accumulate(0, lambda b: mm(wide(0, b), out_weight[columns(b), :]))
+    swap_q.wait_recv()
+    work_q.one()
+    work_q.two()
+    work_q.three()
+    net_k.step4()
+    net_v.step4()
+    work_h.four()
+    accumulate(1, lambda b: transposed(1, 2, b))
     swap_encs.wait_recv()
     side_t[2, :, 0:256] = encs[y, c].T
     side_t[2, :, 256:512] = encs[y, 1 - c].T
-    work_h.four()
-    accumulate(1, lambda b: transposed(1, 2, b))
-    net_v.step4()
-    swap_q.wait_recv()
-    work_q.one()
-    copies.flush([swap_dense_v, swap_dense_k])
-    turn(hids, store_hids)
-    work_h.store()
-    work_q.two()
-    moves_q = exchange_queries()
-    net_k.step4()
-    work_q.three()
-    net_v.done()
-    moves_v = exchange_values()
+    work_q.ring.second()
+    net_k.done()
+    swap_k = swap_half(1)
     for move in moves_q:
         move.wait_recv()
     net_sq.step1()
-    net_k.done()
-    swap_k = swap_half(1)
+    net_v.done()
+    moves_v = exchange_values()
+    net_sq.step2()
+    swap_k.wait_recv()
+    work_k.one()
+    work_q.four()
     for move in moves_v:
         move.wait_recv()
     net_sv.step1()
-    work_q.ring.second()
+    work_k.two()
+    net_sq.step3()
+    work_k.three()
+    copies.flush([swap_dense_v, swap_dense_k])
+    turn(hids, store_hids)
+    net_sv.step2()
     accumulate(2, lambda b: transposed(3, 1, b), last=False)
-    net_sq.step2()
-    swap_k.wait_recv()
-    work_k.one()
-    net_sv.step2()
-    net_sq.step3()
-    work_k.two()
-    work_k.three()
-    work_q.four()
     net_sv.step3()
+    work_k.ring.second()
+    work_h.store()
+    work_k.four()
     net_sq.step4()
-    work_k.ring.second()
-    work_k.four()
+    work_q.store()
     turn(encs, store_encs)
-    accumulate(0, lambda b: mm(wide(0, b), out_weight[columns(b), :]))
     net_sv.step4()
-    work_q.store()
+    net_sq.done()
     accumulate(2, lambda b: transposed(2, 0, b), add=True)
-    net_sq.done()
     grads_out[0, :, 256:512] = whole_grad(turned_hids, query_rows)
     net_sv.done()
     results[3].start()
@@ -954,8 +973,8 @@
             pltpu.VMEM((3, 256, 512), F32),
             pltpu.VMEM((4, 512, 512), F32),
             dma((14,)),
-            dma((256,)),
-            dma((256,)),
+            dma((352,)),
+            dma((352,)),
         ],
         compiler_params=pltpu.CompilerParams(
             collective_id=0, has_side_effects=True, vmem_limit_bytes=limit

time: 143 us -> 140 us (0.979)
  Pallas kernels: 142 us -> 139 us
    pallas_call x1, Pallas kernels: 137 us -> 134 us  [per_device(): pl.pallas_call(layer_kernel, out_shape=results, in_specs=[pl.BlockSpec(me...]
where the time goes in v5:
time: 140 us
  Pallas kernels  139 us (99%)
    pallas_call x1, Pallas kernels, per_device(): pl.pallas_call(layer_kernel, out_shape=results, in_specs=[pl.BlockSpec(me...  134 us
    pallas_call x1, Pallas kernels, per_device(): pl.pallas_call(copy_kernel, out_shape=results, in_specs=[hbm()] * 7, out_...  5.07 us

profile of v5, /device:TPU:0, one launch (start us, length us, event | category | flops | bytes accessed | tf_op | source)
XLA Modules:
  0.0 139.9 jit_solution(17419831467088681981)
XLA Ops:
  0.6 134.0 %shard_map.144 = (f32[256,512]{1,0:T(8,128)}, f32[256,512]{1,0:T(8,128)}, f32[256,512]{1,0:T(8,128)}, f32[512,512]{1,0:T(8,128)}, f32[512,512]{1,0:T(8,128)}, /*index=5*/f32[512,512]{1,0:T(8,128)}, f32[512,512]{1,0:T(8,128)}) custom-call(s32[2,4]{1,0:T(2,128)} %bitcast.4, s32[16]{0:T(128)} %blocks.1, bf16[256,512]{1,0:T(8,128)(2,1)} %hidden.1, ...), custom_call_target="tpu_custom_call" | custom-call | tf_op jit(solution)/shard_map/pallas_call | solution.py:938
  134.7 5.1 %shard_map.145 = (f32[256,512]{1,0:T(8,128)}, f32[256,512]{1,0:T(8,128)}, f32[256,512]{1,0:T(8,128)}, f32[512,512]{1,0:T(8,128)}, f32[512,512]{1,0:T(8,128)}, /*index=5*/f32[512,512]{1,0:T(8,128)}, f32[512,512]{1,0:T(8,128)}) custom-call(f32[256,512]{1,0:T(8,128)} %get-tuple-element.21.refs_0_, f32[256,512]{1,0:T(8,128)} %get-tuple-element.22.refs_1_, ...), custom_call_target="tpu_custom_call" | custom-call | tf_op jit(solution)/shard_map/pallas_call | solution.py:993

commit v6 on v5

--- a/solution.py
+++ b/solution.py
@@ -747,53 +747,61 @@
     first_terms()
     place.meet(met)
     keys.opposite()
+    gather_hids.first()
+    keys.sides()
     make_terms(1)
+    keys.step2()
     values.opposite()
-    keys.sides()
-    gather_hids.first()
-    keys.step2()
-    values.sides()
-    make_terms(2)
-    gather_hids.second()
-    values.step2()
     make_grad_terms()
     gather_encs.first()
+    values.sides()
+    gather_hids.second()
     keys.step3()
+    make_terms(2)
+    values.step2()
+    keys.step4()
     query.opposite()
-    keys.step4()
     values.step3()
+    keys.finish(store_pair(0))
     query.sides()
-    keys.finish(store_pair(0))
     gather_encs.second()
+    gather_keys.first()
     values.step4()
-    gather_keys.first()
+    swap_hids = swap(gather_hids, hids.at[:, c])
     query.step2()
+    grad.opposite()
     values.finish(store_pair(1))
+    gather_keys.second()
+    swap_cots = copies.start(cots.at[0], cots.at[1], place.partner)
     gather_values.first()
-    grad.opposite()
     grad.sides()
-    gather_keys.second()
     query.step3()
+    swap_cots.wait_recv()
+    for k in (0, 1):
+        side_t[0, :, k * 256 : k * 256 + 256] = cots[k].T
+    grad.step2()
+    swap_keys = swap(gather_keys, pair.at[0, :, c])
     gather_values.second()
-    grad.step2()
     query.step4()
+    swap_encs = swap(gather_encs, encs.at[:, c])
     swap_values = swap(gather_values, pair.at[1, :, c])
-    swap_keys = swap(gather_keys, pair.at[0, :, c])
     grad.step3()
     query.finish(store_to(queries))
     swap_keys.wait_recv()
     swap_values.wait_recv()
     attend()
+    grad.step4()
     net_h.step1()
-    swap_hids = swap(gather_hids, hids.at[:, c])
-    grad.step4()
-    net_h.step2()
+    swap_hids.wait_recv()
+    side_t[1, :, 0:256] = hids[y, c].T
+    side_t[1, :, 256:512] = hids[y, 1 - c].T
     flip(prob)
     grad.finish(store_to(grads))
+    net_h.step2()
+    attend_back()
     for total in (keys, values, query, grad):
         for ring in total.two:
             ring.flush()
-    attend_back()
     net_h.step3()
     neighbour_grads(1, grads)
     swap_dense_v = swap_dense(1)
@@ -804,83 +812,75 @@
     net_h.step4()
     moves_dv = send_dense(1, swap_dense_v)
     net_q.step2()
-    swap_cots = copies.start(cots.at[0], cots.at[1], place.partner)
     moves_dk = send_dense(0, swap_dense_k)
+    swap_encs.wait_recv()
+    side_t[2, :, 0:256] = encs[y, c].T
+    side_t[2, :, 256:512] = encs[y, 1 - c].T
     net_h.done()
     swap_h = swap_half(0)
     net_q.step3()
-    swap_cots.wait_recv()
-    for k in (0, 1):
-        side_t[0, :, k * 256 : k * 256 + 256] = cots[k].T
     sum_dense(1, moves_dv)
-    swap_hids.wait_recv()
-    side_t[1, :, 0:256] = hids[y, c].T
-    side_t[1, :, 256:512] = hids[y, 1 - c].T
     net_v.step1()
     swap_h.wait_recv()
     work_h.one()
     net_q.step4()
-    work_h.two()
     gather_keys.flush()
     gather_values.flush()
     copies.flush([swap_keys, swap_values])
     sum_dense(0, moves_dk)
+    work_h.two()
     net_k.step1()
+    net_v.step2()
     work_h.three()
     net_q.done()
-    net_v.step2()
-    swap_encs = swap(gather_encs, encs.at[:, c])
-    work_h.ring.second()
-    net_k.step2()
     moves_q = exchange_queries()
     swap_q = copies.start(terms.at[1, :, 2 * (1 - c)], theirs_q, place.partner)
-    net_k.step3()
-    net_v.step3()
+    net_k.step2()
+    work_h.ring.second()
     accumulate(0, lambda b: mm(wide(0, b), out_weight[columns(b), :]))
     swap_q.wait_recv()
     work_q.one()
     work_q.two()
+    net_k.step3()
+    net_v.step3()
+    copies.flush([swap_dense_v, swap_dense_k])
+    turn(hids, store_hids)
+    work_h.four()
+    turn(encs, store_encs)
     work_q.three()
     net_k.step4()
     net_v.step4()
-    work_h.four()
-    accumulate(1, lambda b: transposed(1, 2, b))
-    swap_encs.wait_recv()
-    side_t[2, :, 0:256] = encs[y, c].T
-    side_t[2, :, 256:512] = encs[y, 1 - c].T
-    work_q.ring.second()
-    net_k.done()
-    swap_k = swap_half(1)
     for move in moves_q:
         move.wait_recv()
     net_sq.step1()
+    accumulate(1, lambda b: transposed(1, 2, b))
+    work_q.ring.second()
+    net_k.done()
+    work_q.four()
+    swap_k = swap_half(1)
     net_v.done()
     moves_v = exchange_values()
     net_sq.step2()
     swap_k.wait_recv()
     work_k.one()
-    work_q.four()
     for move in moves_v:
         move.wait_recv()
     net_sv.step1()
     work_k.two()
     net_sq.step3()
     work_k.three()
-    copies.flush([swap_dense_v, swap_dense_k])
-    turn(hids, store_hids)
+    work_h.store()
     net_sv.step2()
-    accumulate(2, lambda b: transposed(3, 1, b), last=False)
     net_sv.step3()
     work_k.ring.second()
-    work_h.store()
-    work_k.four()
+    work_q.store()
     net_sq.step4()
-    work_q.store()
-    turn(encs, store_encs)
+    accumulate(2, lambda b: transposed(3, 1, b), last=False)
     net_sv.step4()
     net_sq.done()
+    work_k.four()
+    grads_out[0, :, 256:512] = whole_grad(turned_hids, query_rows)
     accumulate(2, lambda b: transposed(2, 0, b), add=True)
-    grads_out[0, :, 256:512] = whole_grad(turned_hids, query_rows)
     net_sv.done()
     results[3].start()
     grads_out[2] = whole_grad(turned_encs, value_rows)

time: 140 us -> 140 us (level)
  no operation moved by 1% of the time
where the time goes in v6:
time: 140 us
  Pallas kernels  139 us (99%)
    pallas_call x1, Pallas kernels, per_device(): pl.pallas_call(layer_kernel, out_shape=results, in_specs=[pl.BlockSpec(me...  134 us
    pallas_call x1, Pallas kernels, per_device(): pl.pallas_call(copy_kernel, out_shape=results, in_specs=[hbm()] * 7, out_...  5.07 us

profile of v6, /device:TPU:0, one launch (start us, length us, event | category | flops | bytes accessed | tf_op | source)
XLA Modules:
  0.0 139.7 jit_solution(3907526694760945940)
XLA Ops:
  0.6 133.8 %shard_map.144 = (f32[256,512]{1,0:T(8,128)}, f32[256,512]{1,0:T(8,128)}, f32[256,512]{1,0:T(8,128)}, f32[512,512]{1,0:T(8,128)}, f32[512,512]{1,0:T(8,128)}, /*index=5*/f32[512,512]{1,0:T(8,128)}, f32[512,512]{1,0:T(8,128)}) custom-call(s32[2,4]{1,0:T(2,128)} %bitcast.4, s32[16]{0:T(128)} %blocks.1, bf16[256,512]{1,0:T(8,128)(2,1)} %hidden.1, ...), custom_call_target="tpu_custom_call" | custom-call | tf_op jit(solution)/shard_map/pallas_call | solution.py:938
  134.5 5.1 %shard_map.145 = (f32[256,512]{1,0:T(8,128)}, f32[256,512]{1,0:T(8,128)}, f32[256,512]{1,0:T(8,128)}, f32[512,512]{1,0:T(8,128)}, f32[512,512]{1,0:T(8,128)}, /*index=5*/f32[512,512]{1,0:T(8,128)}, f32[512,512]{1,0:T(8,128)}) custom-call(f32[256,512]{1,0:T(8,128)} %get-tuple-element.21.refs_0_, f32[256,512]{1,0:T(8,128)} %get-tuple-element.22.refs_1_, ...), custom_call_target="tpu_custom_call" | custom-call | tf_op jit(solution)/shard_map/pallas_call | solution.py:993
